TPU v7x, 256 devices: a whole 4x4x8 slice. The times are simulated.
256 devices in a mesh: dom: 32 (over y, z), node: 8 (over x, core).
Axes of the slice: x: 4, y: 4, z: 8, core: 2. Of those that a mesh axis runs over, the one named last changes fastest.
Arguments:
- positions: float32 [3, 524288], P(None, ('dom', 'node')), may hold values from -6 to 6
- masses: float32 [524288], P(('dom', 'node')), may hold values from 0.5 to 2
- metric: float32 [6, 524288], P(None, ('dom', 'node')), may hold values from -0.75 to 2.5, as said below
- energy: float32 [524288], P(('dom', 'node')), may hold values from 0.5 to 2
- local_pairs: int32 [4096, 1], P(('dom', 'node')), may hold values from 0 to 15
- ghost_pairs: int32 [256, 32], P(('dom', 'node')), may hold values from 0 to 31, each once within a row
- node_sends: int32 [256, 8, 2], P(('dom', 'node')), may hold values from 0 to 15, as said below
- domain_sends: int32 [256, 2, 8], P(('dom', 'node')), may hold values from 0 to 15, as said below
Outputs:
- final_metric: float32 [6, 524288], P(None, ('dom', 'node'))
- density: float32 [524288], P(('dom', 'node'))
- acceleration: float32 [3, 524288], P(None, ('dom', 'node'))
Inputs may be any that keep to these rules, and one draw needn't show every extreme that they name: `local_pairs`: indices of blocks within the owning device. `ghost_pairs`: each device's row names each of its 32 ghost slots exactly once. `node_sends`: indices of blocks within the sending device; each device sends exactly 2 blocks to each device of its node group, itself included, all 16 of them different blocks. `domain_sends`: indices of blocks within the sending device; row 0 goes to the previous domain, row 1 to the next, exactly 8 different blocks in each row. `metric`: each particle's six numbers form a positive definite symmetric matrix.
All inputs are finite; a program needn't handle non-finite values.
Results may differ from a plain program's by a relative error of at most 0.0001.
Values sent between devices are 32-bit elements; how exact they have to be, the bound alone decides.
No kernel may reach another device: no remote copies, remote signals or barrier semaphores. Data moves between devices by JAX's collectives and lax.ppermute only.
A program may use at most 64 MiB of HBM per device.

v0:
```python
import functools

import jax
import jax.numpy as jnp
from jax import lax
from jax.experimental import pallas as pl
from jax.experimental.pallas import tpu as pltpu
from jax.sharding import PartitionSpec as P

W = 128
NB = 16
ITERS = 3
NODE = 8
REMOTE = 64
PARTS = NB + REMOTE
TILES = 96
KDIM = 64
ADIABATIC = 5.0 / 3.0
TARGET_SCALE = 0.5
RIDGE_TERM = 0.1
BF = jnp.bfloat16
F32 = jnp.float32


def split2(value):
    high = value.astype(BF)
    rest = value - high.astype(F32)
    return high, rest.astype(BF)


def split3(value):
    high = value.astype(BF).astype(F32)
    rest = value - high
    middle = rest.astype(BF).astype(F32)
    return high, middle, rest - middle


def send_tables(gp, ns, ds, inv, sent):
    def place(q, carry):
        inv[gp[0, q]] = q // 2
        return carry

    lax.fori_loop(0, 32, place, 0)

    def node(s, carry):
        for k in range(2):
            sent[4 * s + k] = ns[0, s, k]
            sent[4 * s + 2 + k] = inv[2 * s + k]
        return carry

    lax.fori_loop(0, NODE, node, 0)

    def dom(k, carry):
        for side in range(2):
            sent[32 + 16 * side + k] = ds[0, side, k]
            sent[32 + 16 * side + 8 + k] = inv[16 + 8 * side + k]
        return carry

    lax.fori_loop(0, 8, dom, 0)


def lanes(block):
    return pl.ds(pl.multiple_of(block * W, W), W)


def gather_kernel(gp, ns, ds, pos, mass, node_out, prev_out, next_out, inv, sent):
    send_tables(gp, ns, ds, inv, sent)

    def one(t):
        b = sent[t]
        return pos[:, lanes(b)], mass[pl.ds(b, 1), :]

    for t in range(REMOTE):
        place, weight = one(t)
        if t < 32:
            node_out[t // 4, pl.ds(4 * (t % 4), 3), :] = place
            node_out[t // 4, pl.ds(4 * (t % 4) + 3, 1), :] = weight
        else:
            out = prev_out if t < 48 else next_out
            out[pl.ds(4 * (t % 16), 3), :] = place
            out[pl.ds(4 * (t % 16) + 3, 1), :] = weight


def inverse_parts(m):
    cofactors = (
        m[1] * m[2] - m[5] * m[5],
        m[0] * m[2] - m[4] * m[4],
        m[0] * m[1] - m[3] * m[3],
        m[4] * m[5] - m[3] * m[2],
        m[3] * m[5] - m[4] * m[1],
        m[3] * m[4] - m[0] * m[5],
    )
    return cofactors, m[0] * cofactors[0] + m[3] * cofactors[3] + m[4] * cofactors[4]


def apply_metric(g, r):
    return (
        g[0] * r[0] + g[3] * r[1] + g[4] * r[2],
        g[3] * r[0] + g[1] * r[1] + g[5] * r[2],
        g[4] * r[0] + g[5] * r[1] + g[2] * r[2],
    )


def products(r):
    return (
        r[0] * r[0],
        r[1] * r[1],
        r[2] * r[2],
        r[0] * r[1],
        r[0] * r[2],
        r[1] * r[2],
    )


def reciprocal(value):
    guess = pl.reciprocal(value, approx=True)
    return guess * (2.0 - value * guess)


def main_kernel(
    lp,
    gp,
    ns,
    ds,
    pos,
    mass,
    metric,
    energy,
    node_in,
    prev_in,
    next_in,
    final_metric,
    density_out,
    acc_out,
    node_out,
    prev_out,
    next_out,
    part,
    own,
    stage,
    feat,
    pt,
    fs,
    q,
    sums,
    own_r,
    w3,
    h,
    back,
    acc2,
):
    def fixed(e, carry):
        part[4 * e] = lp[e, 0]
        for k in range(2):
            g = gp[0, 2 * e + k]
            part[4 * e + 1 + k] = jnp.where(
                g < 16, 16 + (g // 2) * 4 + g % 2, jnp.where(g < 24, g + 32, g + 40)
            )
        own[e] = lp[e, 0]
        return carry

    lax.fori_loop(0, NB, fixed, 0)

    def listed(s, carry):
        for k in range(2):
            part[4 * ns[0, s, k] + 3] = 16 + 4 * s + 2 + k
            own[16 + 8 * k + s] = ds[0, k, s]
        return carry

    lax.fori_loop(0, NODE, listed, 0)

    def variable_partner(t):
        if t < 16:
            return t
        return 56 + (t - 16) if t < 24 else 72 + (t - 24)

    for e in range(NB):
        own_r[0:3, e, :] = pos[:, e * W : (e + 1) * W]
        own_r[3:9, e, :] = metric[:, e * W : (e + 1) * W]
    r = [own_r[c] for c in range(3)]
    mass_own = mass[...]

    stage[...] = jnp.zeros(stage.shape, F32)
    feat[...] = jnp.zeros(feat.shape, F32)
    ones = jnp.ones((NB, W), F32)

    def spread(blocks, place, weight):
        n = place[0].shape[0]
        values = list(place) + list(products(place))
        for f, value in enumerate(values):
            high, middle, low = split3(value)
            for row, piece in zip((0, 9, 18, 27, 36, 45), (high, high, middle, high, middle, low)):
                stage[0:n, row + f, :] = piece
        for row in (54, 55, 56):
            stage[0:n, row, :] = jnp.ones((n, W), F32)
        for f, value in enumerate([weight] + [weight * v for v in values]):
            high = value.astype(BF).astype(F32)
            feat[0:n, f, :] = high
            feat[0:n, 16 + f, :] = value - high

        def turn(b, carry):
            pt[blocks + b] = jnp.transpose(stage[b]).astype(BF)
            fs[blocks + b] = feat[b].astype(BF)
            return carry

        lax.fori_loop(0, n, turn, 0, unroll=4)

    spread(0, r, mass_own)
    node_view = node_in[...].reshape(32, 4, W)
    prev_view = prev_in[...].reshape(16, 4, W)
    next_view = next_in[...].reshape(16, 4, W)
    for base, view in ((16, node_view), (48, prev_view), (64, next_view)):
        spread(base, [view[:, c, :] for c in range(3)], view[:, 3, :])

    def load_metric():
        return [own_r[3 + c] for c in range(6)]

    def build_q():
        g = load_metric()
        gr = apply_metric(g, r)
        c0 = 1.0 + r[0] * gr[0] + r[1] * gr[1] + r[2] * gr[2]
        coefs = [-2.0 * v for v in gr] + [g[0], g[1], g[2], 2.0 * g[3], 2.0 * g[4], 2.0 * g[5]]
        for f, value in enumerate(coefs):
            high, middle, low = split3(value)
            for row, piece in zip((0, 9, 18, 27, 36, 45), (high, middle, high, low, middle, high)):
                stage[0:NB, row + f, :] = piece
        for row, piece in zip((54, 55, 56), split3(c0)):
            stage[0:NB, row, :] = piece
        for e in range(NB):
            q[e] = stage[e].astype(BF)

    def contract(features, high, middle):
        both = jnp.concatenate([features, features], axis=1)
        out = jnp.dot(
            both, jnp.concatenate([high, middle], axis=0), preferred_element_type=F32
        )
        return out[0:16] + out[16:32]

    def fixed_tiles(body):
        def step(e, carry):
            partners = [part[4 * e + c] for c in range(4)]
            rows = jnp.concatenate([pt[p] for p in partners], axis=0)
            s = jnp.dot(rows, q[e], preferred_element_type=F32)
            features = jnp.concatenate([fs[p] for p in partners], axis=1)
            body(e, s, features)
            return carry

        lax.fori_loop(0, NB, step, 0, unroll=2)

    def variable_tiles(body):
        for t in range(32):
            p = variable_partner(t)
            e = own[t]
            s = jnp.dot(pt[p], q[e], preferred_element_type=F32)
            body(t, e, s, fs[p])

    def moments_fixed(e, s, features):
        weight = reciprocal(s * s)
        sums[e] = contract(features, *split2(weight))

    def moments_variable(t, e, s, features):
        weight = reciprocal(s * s)
        sums[e] = sums[e] + contract(features, *split2(weight))

    for _ in range(ITERS):
        build_q()
        fixed_tiles(moments_fixed)
        variable_tiles(moments_variable)
        m = [sums[:, f, :] for f in range(10)]
        total = m[0]

        def second(a, b, joint):
            return (
                r[a] * r[b] * total - r[a] * m[1 + b] - r[b] * m[1 + a] + m[joint]
            ) / total

        spread_now = [
            second(0, 0, 4) + RIDGE_TERM,
            second(1, 1, 5) + RIDGE_TERM,
            second(2, 2, 6) + RIDGE_TERM,
            second(0, 1, 7),
            second(0, 2, 8),
            second(1, 2, 9),
        ]
        cofactors, determinant = inverse_parts(spread_now)
        g = load_metric()
        for c in range(6):
            own_r[3 + c] = 0.5 * g[c] + 0.5 * TARGET_SCALE * cofactors[c] / determinant

    build_q()

    def final_parts(s, features, width):
        inv1 = reciprocal(s)
        inv2 = inv1 * inv1
        high3, middle3 = split2(inv2 * inv1)
        return contract(features, *split2(inv2)), contract(features, high3, middle3), high3, middle3

    def final_fixed(e, s, features):
        dens, force, high3, middle3 = final_parts(s, features, 4 * W)
        sums[e] = jnp.concatenate([dens[0:8], force[0:8]], axis=0)
        for c in range(4):
            w3[4 * e + c, :, 0:W] = high3[c * W : (c + 1) * W]
            w3[4 * e + c, :, W:] = middle3[c * W : (c + 1) * W]

    def final_variable(t, e, s, features):
        dens, force, high3, middle3 = final_parts(s, features, W)
        sums[e] = sums[e] + jnp.concatenate([dens[0:8], force[0:8]], axis=0)
        w3[64 + t, :, 0:W] = high3
        w3[64 + t, :, W:] = middle3

    fixed_tiles(final_fixed)
    variable_tiles(final_variable)

    g = load_metric()
    _, determinant = inverse_parts(g)
    volume = jnp.sqrt(determinant) / 384.0
    density = volume * sums[:, 0, :]
    density_out[...] = density
    coefficient = (ADIABATIC - 1.0) * energy[...] / density * volume
    for e in range(NB):
        final_metric[:, e * W : (e + 1) * W] = own_r[3:9, e, :]
    a0 = sums[:, 8, :]
    scale = 4.0 * coefficient
    pull = apply_metric(g, [r[c] * a0 - sums[:, 9 + c, :] for c in range(3)])
    for c in range(3):
        acc2[c] = scale * pull[c]
    scale = scale * mass_own
    feat[...] = jnp.zeros(feat.shape, F32)
    for f, value in enumerate(list(g) + list(apply_metric(g, r))):
        value = scale * value
        high = value.astype(BF).astype(F32)
        feat[0:NB, f, :] = high
        feat[0:NB, 16 + f, :] = value - high
    for e in range(NB):
        h[e] = feat[e].astype(BF)

    back[0:NB] = jnp.zeros((NB, 16, W), F32)

    def turn_back(features, weights):
        both = jnp.concatenate([features, features], axis=1)
        out = lax.dot_general(
            both, weights, (((1,), (1,)), ((), ())), preferred_element_type=F32
        )
        return out[0:16] + out[16:32]

    def back_fixed(e, carry):
        for c in range(4):
            p = part[4 * e + c]
            out = turn_back(h[e], w3[4 * e + c])
            if c == 0:
                back[p] = back[p] + out
            else:
                back[p] = out
        return carry

    lax.fori_loop(0, NB, back_fixed, 0, unroll=2)
    for t in range(32):
        p = variable_partner(t)
        out = turn_back(h[own[t]], w3[64 + t])
        if t < 16:
            back[p] = back[p] + out
        else:
            back[p] = out

    def push(first, count, place):
        b = [back[first : first + count, f, :] for f in range(9)]
        moved = apply_metric(b, place)
        return [moved[c] - b[6 + c] for c in range(3)]

    local = push(0, NB, r)
    for c in range(3):
        acc_out[c] = acc2[c] + local[c]
    for first, count, view, out in (
        (16, 32, node_view, node_out),
        (48, 16, prev_view, prev_out),
        (64, 16, next_view, next_out),
    ):
        place = [view[:, c, :] for c in range(3)]
        values = push(first, count, place)
        for c in range(3):
            out[:, c, :] = values[c]
        out[:, 3, :] = jnp.zeros((count, W), F32)


def final_kernel(gp, ns, ds, acc_in, node_in, prev_in, next_in, out, inv, sent, acc):
    send_tables(gp, ns, ds, inv, sent)
    for c in range(3):
        acc[:, c, :] = acc_in[c]
    acc[:, 3, :] = jnp.zeros((NB, W), F32)
    for t in range(REMOTE):
        b = sent[t]
        if t < 32:
            value = node_in[t // 4, pl.ds(4 * (t % 4), 4), :]
        else:
            value = (prev_in if t < 48 else next_in)[pl.ds(4 * (t % 16), 4), :]
        acc[b] = acc[b] + value
    for e in range(NB):
        out[:, e * W : (e + 1) * W] = acc[e, 0:3, :]


SMEM = pl.BlockSpec(memory_space=pltpu.SMEM)
VMEM = pl.BlockSpec(memory_space=pltpu.VMEM)
PARAMS = pltpu.CompilerParams(vmem_limit_bytes=48 * 1024 * 1024)


def shape(*dims):
    return jax.ShapeDtypeStruct(dims, F32)


def gather_call(gp, ns, ds, pos, mass):
    return pl.pallas_call(
        gather_kernel,
        out_shape=(shape(NODE, 16, W), shape(64, W), shape(64, W)),
        in_specs=[SMEM] * 3 + [VMEM] * 2,
        out_specs=(VMEM,) * 3,
        scratch_shapes=[pltpu.SMEM((32,), jnp.int32), pltpu.SMEM((REMOTE,), jnp.int32)],
        compiler_params=PARAMS,
    )(gp, ns, ds, pos, mass)


def main_call(lp, gp, ns, ds, pos, mass, metric, energy, node_in, prev_in, next_in):
    return pl.pallas_call(
        main_kernel,
        out_shape=(
            shape(6, NB * W),
            shape(NB, W),
            shape(3, NB, W),
            shape(32, 4, W),
            shape(16, 4, W),
            shape(16, 4, W),
        ),
        in_specs=[SMEM] * 4 + [VMEM] * 7,
        out_specs=(VMEM,) * 6,
        scratch_shapes=[
            pltpu.SMEM((64,), jnp.int32),
            pltpu.SMEM((32,), jnp.int32),
            pltpu.VMEM((32, KDIM, W), F32),
            pltpu.VMEM((32, 32, W), F32),
            pltpu.VMEM((PARTS, W, KDIM), BF),
            pltpu.VMEM((PARTS, 32, W), BF),
            pltpu.VMEM((NB, KDIM, W), BF),
            pltpu.VMEM((NB, 16, W), F32),
            pltpu.VMEM((9, NB, W), F32),
            pltpu.VMEM((TILES, W, 2 * W), BF),
            pltpu.VMEM((NB, 32, W), BF),
            pltpu.VMEM((PARTS, 16, W), F32),
            pltpu.VMEM((3, NB, W), F32),
        ],
        compiler_params=PARAMS,
    )(lp, gp, ns, ds, pos, mass, metric, energy, node_in, prev_in, next_in)


def final_call(gp, ns, ds, acc, node_in, prev_in, next_in):
    return pl.pallas_call(
        final_kernel,
        out_shape=shape(3, NB * W),
        in_specs=[SMEM] * 3 + [VMEM] * 4,
        out_specs=VMEM,
        scratch_shapes=[
            pltpu.SMEM((32,), jnp.int32),
            pltpu.SMEM((REMOTE,), jnp.int32),
            pltpu.VMEM((NB, 4, W), F32),
        ],
        compiler_params=PARAMS,
    )(gp, ns, ds, acc, node_in, prev_in, next_in)


def exchange(node, to_prev, to_next, domains):
    up = [(i, i + 1) for i in range(domains - 1)]
    down = [(i + 1, i) for i in range(domains - 1)]
    node_in = lax.all_to_all(node, "node", split_axis=0, concat_axis=0, tiled=True)
    prev_in = lax.ppermute(to_next, "dom", up)
    next_in = lax.ppermute(to_prev, "dom", down)
    return node_in, prev_in, next_in


def on_device(
    domains, positions, masses, metric, energy, local_pairs, ghost_pairs, node_sends, domain_sends
):
    tables = (ghost_pairs, node_sends, domain_sends)
    mass = masses.reshape(NB, W)
    received = exchange(*gather_call(*tables, positions, mass), domains)
    out_metric, density, acc, node, to_prev, to_next = main_call(
        local_pairs, *tables, positions, mass, metric, energy.reshape(NB, W), *received
    )
    returned = exchange(
        node.reshape(NODE, 16, W), to_prev.reshape(64, W), to_next.reshape(64, W), domains
    )
    acceleration = final_call(*tables, acc, *returned)
    return out_metric, density.reshape(-1), acceleration


def solution(mesh):
    both = ("dom", "node")
    in_specs = (
        P(None, both),
        P(both),
        P(None, both),
        P(both),
        P(both, None),
        P(both, None),
        P(both, None, None),
        P(both, None, None),
    )
    out_specs = (P(None, both), P(both), P(None, both))
    return jax.shard_map(
        functools.partial(on_device, mesh.shape["dom"]),
        mesh=mesh,
        in_specs=in_specs,
        out_specs=out_specs,
        check_vma=False,
    )
```

profile of v0, /device:TPU:26, one launch (start us, length us, event | category | flops | bytes accessed | tf_op | source)
XLA Modules:
  0.0 72.7 jit_solution(2026784085672782679)
XLA Ops:
  0.6 0.8 %copy.13.ns = s32[1,8,2]{2,1,0:T(8,128)S(1)} copy(s32[1,8,2]{1,2,0:T(2,128)} %param.14) | data formatting | bytes 128 | tf_op args[6]
  1.4 0.0 copy-start.5
  1.4 0.0 copy-start.7
  1.4 0.7 copy-done.5
  2.1 0.0 copy-done.7
  2.1 0.0 copy-start
  2.1 0.8 %copy-done = f32[3,2048]{1,0:T(4,128)S(1)} copy-done((f32[3,2048]{1,0:T(4,128)S(1)}, f32[3,2048]{1,0:T(4,128)}, u32[]{:S(2)}) %copy-start) | copy-done | bytes 24600
  2.8 0.7 copy-done.3
  3.5 1.8 %shard_map.103 = (f32[8,16,128]{2,1,0:T(8,128)}, f32[64,128]{1,0:T(8,128)S(1)}, f32[64,128]{1,0:T(8,128)S(1)}) custom-call(s32[1,32]{1,0:T(1,128)S(1)} %copy-done.7, s32[1,8,2]{2,1,0:T(8,128)S(1)} %copy.13.ns, s32[1,2,8]{2,1,0:T(2,128)S(1)} %copy-done.5, f32[3,2048]{1,0:T(4,128)S(1)} %copy-done, f32[16,128]{1,0:T(8,128)S(1)} %bitcast.6), custom_call_target="tpu_custom_call" | custom-call | tf_op jit(solution)/shard_map/pallas_call | solution.py:411
  5.3 0.0 copy-start.1
  5.3 0.0 copy-start.2
  5.3 0.0 copy-start.6
  5.3 5.0 %all-to-all-start = ((f32[8,16,128]{2,1,0:T(8,128)}), f32[8,16,128]{2,1,0:T(8,128)S(1)}, u32[]{:S(2)}, u32[]{:S(2)}) async-start(f32[8,16,128]{2,1,0:T(8,128)} %get-tuple-element.12), calls=%async_computation | async-start | bytes 131072 | tf_op jit(solution)/shard_map/all_to_all | solution.py:471
  10.3 3.9 %collective-permute-start = (f32[64,128]{1,0:T(8,128)S(1)}, f32[64,128]{1,0:T(8,128)S(1)}, u32[]{:S(2)}, u32[]{:S(2)}) collective-permute-start(f32[64,128]{1,0:T(8,128)S(1)} %get-tuple-element.13), channel_id=1, source_target_pairs={{0,8},{8,16},{16,24},{24,32},{32,40},{40,48},{48,56},{56,64},{64,7... | collective-permute-start | bytes 98312 | tf_op jit(solution)/shard_map/ppermute | solution.py:472
  14.3 6.0 %collective-permute-start.1 = (f32[64,128]{1,0:T(8,128)S(1)}, f32[64,128]{1,0:T(8,128)S(1)}, u32[]{:S(2)}, u32[]{:S(2)}) collective-permute-start(f32[64,128]{1,0:T(8,128)S(1)} %get-tuple-element.14), channel_id=1, source_target_pairs={{8,0},{16,8},{24,16},{32,24},{40,32},{48,40},{56,48},{64,56},{72,6... | collective-permute-start | bytes 98312 | tf_op jit(solution)/shard_map/ppermute | solution.py:473
  20.3 0.0 copy-done.8
  20.3 0.1 copy.12.lp
  20.4 0.0 collective-permute-done.prev_in
  20.4 1.5 %collective-permute-done.1.next_in = f32[64,128]{1,0:T(8,128)S(1)} collective-permute-done((f32[64,128]{1,0:T(8,128)S(1)}, f32[64,128]{1,0:T(8,128)S(1)}, u32[]{:S(2)}, u32[]{:S(2)}) %collective-permute-start.1) | collective-permute-done | bytes 32800 | tf_op jit(solution)/shard_map/ppermute | solution.py:473
  21.9 0.0 all-to-all-done.node_in
  21.9 0.0 copy-done.1
  21.9 0.0 copy-done.2
  21.9 0.0 copy-done.6
  21.9 0.0 copy-done.4
  21.9 34.2 %shard_map.104 = (f32[6,2048]{1,0:T(8,128)}, f32[16,128]{1,0:T(8,128)}, f32[3,16,128]{2,1,0:T(8,128)S(1)}, f32[32,4,128]{2,1,0:T(4,128)}, f32[16,4,128]{2,1,0:T(4,128)S(1)}, /*index=5*/f32[16,4,128]{2,1,0:T(4,128)S(1)}) custom-call(s32[16,1]{1,0:T(8,128)S(1)} %copy.12.lp, s32[1,32]{1,0:T(1,128)S(1)} %copy-done.7, s32[1,8,2]{2,1,0:T(8,128)S(1)} %copy.13.ns, ...), custom_call_target="tpu_custom_call" | custom-call | tf_op jit(solution)/shard_map/pallas_call | solution.py:422
  56.1 4.8 %all-to-all-start.1 = ((f32[8,16,128]{2,1,0:T(8,128)}), f32[8,16,128]{2,1,0:T(8,128)S(1)}, u32[]{:S(2)}, u32[]{:S(2)}) async-start(f32[8,16,128]{2,1,0:T(8,128)} %bitcast.3), calls=%async_computation.1 | async-start | bytes 131072 | tf_op jit(solution)/shard_map/all_to_all | solution.py:471
  60.9 2.0 %collective-permute-start.2 = (f32[64,128]{1,0:T(8,128)S(1)}, f32[64,128]{1,0:T(8,128)S(1)}, u32[]{:S(2)}, u32[]{:S(2)}) collective-permute-start(f32[64,128]{1,0:T(8,128)S(1)} %bitcast.10), channel_id=1, source_target_pairs={{0,8},{8,16},{16,24},{24,32},{32,40},{40,48},{48,56},{56,64},{64,7... | collective-permute-start | bytes 98312 | tf_op jit(solution)/shard_map/ppermute | solution.py:472
  63.0 6.2 %collective-permute-start.3 = (f32[64,128]{1,0:T(8,128)S(1)}, f32[64,128]{1,0:T(8,128)S(1)}, u32[]{:S(2)}, u32[]{:S(2)}) collective-permute-start(f32[64,128]{1,0:T(8,128)S(1)} %bitcast.9), channel_id=1, source_target_pairs={{8,0},{16,8},{24,16},{32,24},{40,32},{48,40},{56,48},{64,56},{72,6... | collective-permute-start | bytes 98312 | tf_op jit(solution)/shard_map/ppermute | solution.py:473
  69.2 0.0 collective-permute-done.2.prev_in
  69.2 1.6 %collective-permute-done.3.next_in = f32[64,128]{1,0:T(8,128)S(1)} collective-permute-done((f32[64,128]{1,0:T(8,128)S(1)}, f32[64,128]{1,0:T(8,128)S(1)}, u32[]{:S(2)}, u32[]{:S(2)}) %collective-permute-start.3) | collective-permute-done | bytes 32800 | tf_op jit(solution)/shard_map/ppermute | solution.py:473
  70.8 0.0 all-to-all-done.1.node_in
  70.8 1.9 %shard_map.105 = f32[3,2048]{1,0:T(4,128)} custom-call(s32[1,32]{1,0:T(1,128)S(1)} %copy-done.7, s32[1,8,2]{2,1,0:T(8,128)S(1)} %copy.13.ns, s32[1,2,8]{2,1,0:T(2,128)S(1)} %copy-done.5, f32[3,16,128]{2,1,0:T(8,128)S(1)} %get-tuple-element.17.acc_in, f32[8,16,128]{2,1,0:T(8,128)S(1)} %all-to-all-done.1.node_in, ...), custom_call_target="tpu_custom_call" | custom-call | tf_op jit(solution)/shard_map/pallas_call | solution.py:454
  (3 shorter events, 0.0 us)
Async XLA Ops:
  1.4 0.7 copy-start.5
  1.4 0.7 copy-start.7
  2.1 0.8 %copy-start = (f32[3,2048]{1,0:T(4,128)S(1)}, f32[3,2048]{1,0:T(4,128)}, u32[]{:S(2)}) copy-start(f32[3,2048]{1,0:T(4,128)} %pos.3) | copy-start | bytes 73732
  2.8 0.7 copy-start.3
  5.3 15.0 %copy-start.8 = (s32[16,1]{0,1:T(1,128)S(1)}, s32[16,1]{0,1:T(1,128)}, u32[]{:S(2)}) copy-start(s32[16,1]{0,1:T(1,128)} %param.12) | copy-start | bytes 196
  5.3 16.6 %copy-start.1 = (f32[3,2048]{1,0:T(4,128)S(1)}, f32[3,2048]{1,0:T(4,128)}, u32[]{:S(2)}) copy-start(f32[3,2048]{1,0:T(4,128)} %pos.3) | copy-start | bytes 73732
  5.3 16.6 %copy-start.2 = (f32[6,2048]{1,0:T(8,128)S(1)}, f32[6,2048]{1,0:T(8,128)}, u32[]{:S(2)}) copy-start(f32[6,2048]{1,0:T(8,128)} %metric.1) | copy-start | bytes 147460
  5.3 16.6 %copy-start.6 = (f32[2048]{0:T(1024)S(1)}, f32[2048]{0:T(1024)}, u32[]{:S(2)}) copy-start(f32[2048]{0:T(1024)} %param.11) | copy-start | bytes 24580
  5.3 16.6 %all-to-all-start = ((f32[8,16,128]{2,1,0:T(8,128)}), f32[8,16,128]{2,1,0:T(8,128)S(1)}, u32[]{:S(2)}, u32[]{:S(2)}) async-start(f32[8,16,128]{2,1,0:T(8,128)} %get-tuple-element.12), calls=%async_computation | async-start | bytes 131072 | tf_op jit(solution)/shard_map/all_to_all | solution.py:471
  10.3 11.6 %copy-start.4 = (f32[2048]{0:T(1024)S(1)}, f32[2048]{0:T(1024)}, u32[]{:S(2)}) copy-start(f32[2048]{0:T(1024)} %param.9) | copy-start | bytes 24580
  10.3 10.1 %collective-permute-start = (f32[64,128]{1,0:T(8,128)S(1)}, f32[64,128]{1,0:T(8,128)S(1)}, u32[]{:S(2)}, u32[]{:S(2)}) collective-permute-start(f32[64,128]{1,0:T(8,128)S(1)} %get-tuple-element.13), channel_id=1, source_target_pairs={{0,8},{8,16},{16,24},{24,32},{32,40},{40,48},{48,56},{56,64},{64,7... | collective-permute-start | bytes 98312 | tf_op jit(solution)/shard_map/ppermute | solution.py:472
  14.3 7.6 %collective-permute-start.1 = (f32[64,128]{1,0:T(8,128)S(1)}, f32[64,128]{1,0:T(8,128)S(1)}, u32[]{:S(2)}, u32[]{:S(2)}) collective-permute-start(f32[64,128]{1,0:T(8,128)S(1)} %get-tuple-element.14), channel_id=1, source_target_pairs={{8,0},{16,8},{24,16},{32,24},{40,32},{48,40},{56,48},{64,56},{72,6... | collective-permute-start | bytes 98312 | tf_op jit(solution)/shard_map/ppermute | solution.py:473
  56.1 14.7 %all-to-all-start.1 = ((f32[8,16,128]{2,1,0:T(8,128)}), f32[8,16,128]{2,1,0:T(8,128)S(1)}, u32[]{:S(2)}, u32[]{:S(2)}) async-start(f32[8,16,128]{2,1,0:T(8,128)} %bitcast.3), calls=%async_computation.1 | async-start | bytes 131072 | tf_op jit(solution)/shard_map/all_to_all | solution.py:471
  60.9 8.3 %collective-permute-start.2 = (f32[64,128]{1,0:T(8,128)S(1)}, f32[64,128]{1,0:T(8,128)S(1)}, u32[]{:S(2)}, u32[]{:S(2)}) collective-permute-start(f32[64,128]{1,0:T(8,128)S(1)} %bitcast.10), channel_id=1, source_target_pairs={{0,8},{8,16},{16,24},{24,32},{32,40},{40,48},{48,56},{56,64},{64,7... | collective-permute-start | bytes 98312 | tf_op jit(solution)/shard_map/ppermute | solution.py:472
  63.0 7.8 %collective-permute-start.3 = (f32[64,128]{1,0:T(8,128)S(1)}, f32[64,128]{1,0:T(8,128)S(1)}, u32[]{:S(2)}, u32[]{:S(2)}) collective-permute-start(f32[64,128]{1,0:T(8,128)S(1)} %bitcast.9), channel_id=1, source_target_pairs={{8,0},{16,8},{24,16},{32,24},{40,32},{48,40},{56,48},{64,56},{72,6... | collective-permute-start | bytes 98312 | tf_op jit(solution)/shard_map/ppermute | solution.py:473
where the time goes:
time: 73.7 us; the launch traced here: 72.7 us
  Pallas kernels  38 us (52%)
  starting transfers between devices  28 us (38%)
  waiting for transfers between devices  3.05 us (4%)
  local copies, waits for them, and re-layouts  2.99 us (4%)
    pallas_call x1, Pallas kernels, main_call(): pl.pallas_call(main_kernel, out_shape=(shape(6, NB * W), shape(NB, W), sh...  34.2 us
    ppermute x2, starting transfers between devices, exchange(): next_in = lax.ppermute(to_prev, 'dom', down)  12.3 us
    all_to_all x2, starting transfers between devices, exchange(): lax.all_to_all(node, 'node', split_axis=0, concat_axis=0, tiled=True)  9.79 us
    ppermute x2, starting transfers between devices, exchange(): prev_in = lax.ppermute(to_next, 'dom', up)  5.95 us
    ppermute x2, waiting for transfers between devices, exchange(): next_in = lax.ppermute(to_prev, 'dom', down)  3.04 us
    unnamed x20, local copies, waits for them, and re-layouts  2.99 us
    pallas_call x1, Pallas kernels, final_call(): pl.pallas_call(final_kernel, out_shape=shape(3, NB * W), in_specs=[SMEM]...  1.94 us
    pallas_call x1, Pallas kernels, gather_call(): pl.pallas_call(gather_kernel, out_shape=(shape(NODE, 16, W), shape(64, W)...  1.8 us
  transfers between devices with their start and end apart: 6, of which 2 were waited for; matrix products, arithmetic and copies ran while one was open for 0% of the time, Pallas kernels for 0%

commit v1 on v0

v1 whole, which is shorter than its diff:
```python
import functools

import jax
import jax.numpy as jnp
from jax import lax
from jax.experimental import pallas as pl
from jax.experimental.pallas import tpu as pltpu
from jax.sharding import PartitionSpec as P

W = 128
NB = 16
ITERS = 3
NODE = 8
REMOTE = 64
PARTS = NB + REMOTE
TILES = 96
KDIM = 64
ADIABATIC = 5.0 / 3.0
TARGET_SCALE = 0.5
RIDGE_TERM = 0.1
BF = jnp.bfloat16
F32 = jnp.float32


def side_of(pairing):
    return lax.rem(lax.axis_index("dom") + pairing + 1, 2)


def split2(value):
    high = value.astype(BF)
    rest = value - high.astype(F32)
    return high, rest.astype(BF)


def split3(value):
    high = value.astype(BF).astype(F32)
    rest = value - high
    middle = rest.astype(BF).astype(F32)
    return high, middle, rest - middle


def send_tables(gp, ns, ds, inv, sent):
    for slot in range(32):
        inv[gp[0, slot]] = slot // 2
    for s in range(NODE):
        for k in range(2):
            sent[4 * s + k] = ns[0, k, s]
            sent[4 * s + 2 + k] = inv[2 * s + k]
    for pairing in range(2):
        side = side_of(pairing)
        for k in range(8):
            sent[32 + 16 * pairing + k] = ds[0, side, k]
            sent[40 + 16 * pairing + k] = inv[16 + 8 * side + k]


def lanes(block):
    return pl.ds(pl.multiple_of(block * W, W), W)


def gather_kernel(
    gp_in, ns_in, ds_in, pos_in, mass_in, node_out, even_out, odd_out,
    gp, ns, ds, pos, mass, inv, sent, sems,
):
    pairs = ((gp_in, gp), (ns_in, ns), (ds_in, ds), (pos_in, pos), (mass_in, mass))
    copies = [
        pltpu.make_async_copy(source, target, sems.at[c])
        for c, (source, target) in enumerate(pairs)
    ]
    for copy in copies:
        copy.start()
    for copy in copies:
        copy.wait()
    send_tables(gp, ns, ds, inv, sent)
    for t in range(REMOTE):
        b = sent[t]
        place, weight = pos[:, lanes(b)], mass[pl.ds(b, 1), :]
        out = node_out.at[t // 4] if t < 32 else (even_out if t < 48 else odd_out)
        row = 4 * (t % 4) if t < 32 else 4 * (t % 16)
        out[row : row + 3, :] = place
        out[row + 3 : row + 4, :] = weight


def inverse_parts(m):
    cofactors = (
        m[1] * m[2] - m[5] * m[5],
        m[0] * m[2] - m[4] * m[4],
        m[0] * m[1] - m[3] * m[3],
        m[4] * m[5] - m[3] * m[2],
        m[3] * m[5] - m[4] * m[1],
        m[3] * m[4] - m[0] * m[5],
    )
    return cofactors, m[0] * cofactors[0] + m[3] * cofactors[3] + m[4] * cofactors[4]


def apply_metric(g, r):
    return (
        g[0] * r[0] + g[3] * r[1] + g[4] * r[2],
        g[3] * r[0] + g[1] * r[1] + g[5] * r[2],
        g[4] * r[0] + g[5] * r[1] + g[2] * r[2],
    )


def products(r):
    return (
        r[0] * r[0],
        r[1] * r[1],
        r[2] * r[2],
        r[0] * r[1],
        r[0] * r[2],
        r[1] * r[2],
    )


def reciprocal(value):
    guess = pl.reciprocal(value, approx=True)
    return guess * (2.0 - value * guess)


def spread(stage, feat, pt, fs, first, place, weight):
    n = place[0].shape[0]
    values = list(place) + list(products(place))
    for f, value in enumerate(values):
        high, middle, low = split3(value)
        for row, piece in zip((0, 9, 18, 27, 36, 45), (high, high, middle, high, middle, low)):
            stage[0:n, row + f, :] = piece
    for row in (54, 55, 56):
        stage[0:n, row, :] = jnp.ones((n, W), F32)
    for row in range(57, KDIM):
        stage[0:n, row, :] = jnp.zeros((n, W), F32)
    for f, value in enumerate([weight] + [weight * v for v in values]):
        high = value.astype(BF).astype(F32)
        feat[0:n, f, :] = high
        feat[0:n, 16 + f, :] = value - high
    for f in range(10, 16):
        feat[0:n, f, :] = jnp.zeros((n, W), F32)
        feat[0:n, 16 + f, :] = jnp.zeros((n, W), F32)
    for b in range(n):
        pt[first + b] = jnp.transpose(stage[b]).astype(BF)
        fs[first + b] = feat[b].astype(BF)


def form_coefficients(g, r):
    gr = apply_metric(g, r)
    constant = 1.0 + r[0] * gr[0] + r[1] * gr[1] + r[2] * gr[2]
    return [constant] + [-2.0 * v for v in gr] + list(g[0:3]) + [2.0 * v for v in g[3:6]]


def build_q(stage, q, g, r):
    constant, *others = form_coefficients(g, r)
    for f, value in enumerate(others):
        high, middle, low = split3(value)
        for row, piece in zip((0, 9, 18, 27, 36, 45), (high, middle, high, low, middle, high)):
            stage[0:NB, row + f, :] = piece
    for row, piece in zip((54, 55, 56), split3(constant)):
        stage[0:NB, row, :] = piece
    for e in range(NB):
        q[e] = stage[e].astype(BF)


def contract(features, high, middle):
    both = jnp.concatenate([features, features], axis=1)
    out = jnp.dot(both, jnp.concatenate([high, middle], axis=0), preferred_element_type=F32)
    return out[0:16] + out[16:32]


def local_kernel(pos, mass, metric, own_r, pt, fs, stage, feat):
    for e in range(NB):
        own_r[0:3, e, :] = pos[:, e * W : (e + 1) * W]
        own_r[3:9, e, :] = metric[:, e * W : (e + 1) * W]
    r = [own_r[c] for c in range(3)]
    spread(stage, feat, pt, fs, 0, r, mass[...])


def main_kernel(
    lp,
    gp,
    ns,
    ds,
    mass,
    energy,
    start_r,
    pt_local,
    fs_local,
    node_in,
    even_in,
    odd_in,
    final_metric,
    density_out,
    acc_out,
    node_out,
    even_out,
    odd_out,
    part,
    own,
    stage,
    feat,
    pt,
    fs,
    q,
    sums,
    own_r,
    w3,
    h,
    back,
    acc2,
):
    for e in range(NB):
        part[4 * e] = lp[0, e]
        own[e] = lp[0, e]
        for k in range(2):
            g = gp[0, 2 * e + k]
            pairing = side_of(g // 8)
            part[4 * e + 1 + k] = jnp.where(
                g < 16, 16 + (g // 2) * 4 + g % 2, 48 + 16 * pairing + g % 8
            )
    for s in range(NODE):
        for k in range(2):
            part[4 * ns[0, k, s] + 3] = 16 + 4 * s + 2 + k
            own[16 + 8 * k + s] = ds[0, side_of(k), s]

    def variable_partner(t):
        if t < 16:
            return t
        return 56 + (t - 16) if t < 24 else 72 + (t - 24)

    own_r[...] = start_r[...]
    pt[0:NB] = pt_local[...]
    fs[0:NB] = fs_local[...]
    r = [own_r[c] for c in range(3)]
    mass_own = mass[...]
    node_view = node_in[...].reshape(32, 4, W)
    even_view = even_in[...].reshape(16, 4, W)
    odd_view = odd_in[...].reshape(16, 4, W)
    for base, view in ((16, node_view), (48, even_view), (64, odd_view)):
        spread(stage, feat, pt, fs, base, [view[:, c, :] for c in range(3)], view[:, 3, :])
    for row in range(57, KDIM):
        stage[0:NB, row, :] = jnp.zeros((NB, W), F32)

    def load_metric():
        return [own_r[3 + c] for c in range(6)]

    def fixed_tiles(body):
        for e in range(NB):
            partners = [part[4 * e + c] for c in range(4)]
            rows = jnp.concatenate([pt[p] for p in partners], axis=0)
            s = jnp.dot(rows, q[e], preferred_element_type=F32)
            features = jnp.concatenate([fs[p] for p in partners], axis=1)
            body(e, s, features)

    def variable_tiles(body):
        for t in range(32):
            p = variable_partner(t)
            e = own[t]
            s = jnp.dot(pt[p], q[e], preferred_element_type=F32)
            body(t, e, s, fs[p])

    def moments_fixed(e, s, features):
        weight = reciprocal(s * s)
        sums[e] = contract(features, *split2(weight))

    def moments_variable(t, e, s, features):
        weight = reciprocal(s * s)
        sums[e] = sums[e] + contract(features, *split2(weight))

    def iteration(_, carry):
        build_q(stage, q, load_metric(), r)
        fixed_tiles(moments_fixed)
        variable_tiles(moments_variable)
        m = [sums[:, f, :] for f in range(10)]
        total = m[0]

        def second(a, b, joint):
            return (
                r[a] * r[b] * total - r[a] * m[1 + b] - r[b] * m[1 + a] + m[joint]
            ) / total

        spread_now = [
            second(0, 0, 4) + RIDGE_TERM,
            second(1, 1, 5) + RIDGE_TERM,
            second(2, 2, 6) + RIDGE_TERM,
            second(0, 1, 7),
            second(0, 2, 8),
            second(1, 2, 9),
        ]
        cofactors, determinant = inverse_parts(spread_now)
        g = load_metric()
        for c in range(6):
            own_r[3 + c] = 0.5 * g[c] + 0.5 * TARGET_SCALE * cofactors[c] / determinant
        return carry

    lax.fori_loop(0, ITERS, iteration, 0)
    g = load_metric()
    build_q(stage, q, g, r)

    def cubes(s):
        inverse = reciprocal(s)
        return split2(inverse * inverse * inverse)

    def final_fixed(e, s, features):
        high3, middle3 = cubes(s)
        sums[e] = contract(features, high3, middle3)
        for c in range(4):
            w3[4 * e + c, :, 0:W] = high3[c * W : (c + 1) * W]
            w3[4 * e + c, :, W:] = middle3[c * W : (c + 1) * W]

    def final_variable(t, e, s, features):
        high3, middle3 = cubes(s)
        sums[e] = sums[e] + contract(features, high3, middle3)
        w3[64 + t, :, 0:W] = high3
        w3[64 + t, :, W:] = middle3

    fixed_tiles(final_fixed)
    variable_tiles(final_variable)

    _, determinant = inverse_parts(g)
    volume = jnp.sqrt(determinant) / 384.0
    m = [sums[:, f, :] for f in range(10)]
    density_sum = 0.0
    for coefficient, value in zip(form_coefficients(g, r), m):
        density_sum = density_sum + coefficient * value
    density = volume * density_sum
    density_out[...] = density
    coefficient = (ADIABATIC - 1.0) * energy[...] / density * volume
    for e in range(NB):
        final_metric[:, e * W : (e + 1) * W] = own_r[3:9, e, :]
    scale = 4.0 * coefficient
    pull = apply_metric(g, [r[c] * m[0] - m[1 + c] for c in range(3)])
    for c in range(3):
        acc2[c] = scale * pull[c]
    scale = scale * mass_own
    for f, value in enumerate(list(g) + list(apply_metric(g, r))):
        value = scale * value
        high = value.astype(BF).astype(F32)
        feat[0:NB, f, :] = high
        feat[0:NB, 16 + f, :] = value - high
    for f in (9, 25):
        feat[0:NB, f, :] = jnp.zeros((NB, W), F32)
    for e in range(NB):
        h[e] = feat[e].astype(BF)

    back[0:NB] = jnp.zeros((NB, 16, W), F32)

    def turn_back(features, weights):
        both = jnp.concatenate([features, features], axis=1)
        out = lax.dot_general(
            both, weights, (((1,), (1,)), ((), ())), preferred_element_type=F32
        )
        return out[0:16] + out[16:32]

    for e in range(NB):
        for c in range(4):
            p = part[4 * e + c]
            out = turn_back(h[e], w3[4 * e + c])
            if c == 0:
                back[p] = back[p] + out
            else:
                back[p] = out
    for t in range(32):
        p = variable_partner(t)
        out = turn_back(h[own[t]], w3[64 + t])
        if t < 16:
            back[p] = back[p] + out
        else:
            back[p] = out

    def push(first, count, place):
        b = [back[first : first + count, f, :] for f in range(9)]
        moved = apply_metric(b, place)
        return [moved[c] - b[6 + c] for c in range(3)]

    local = push(0, NB, r)
    for c in range(3):
        acc_out[c] = acc2[c] + local[c]
    for first, count, view, out in (
        (16, 32, node_view, node_out),
        (48, 16, even_view, even_out),
        (64, 16, odd_view, odd_out),
    ):
        place = [view[:, c, :] for c in range(3)]
        values = push(first, count, place)
        for c in range(3):
            out[:, c, :] = values[c]
        out[:, 3, :] = jnp.zeros((count, W), F32)


def final_kernel(gp, ns, ds, acc_in, node_in, even_in, odd_in, out, inv, sent, acc):
    send_tables(gp, ns, ds, inv, sent)
    for c in range(3):
        acc[:, c, :] = acc_in[c]
    acc[:, 3, :] = jnp.zeros((NB, W), F32)
    for t in range(REMOTE):
        b = sent[t]
        if t < 32:
            value = node_in[t // 4, pl.ds(4 * (t % 4), 4), :]
        else:
            value = (even_in if t < 48 else odd_in)[pl.ds(4 * (t % 16), 4), :]
        acc[b] = acc[b] + value
    for e in range(NB):
        out[:, e * W : (e + 1) * W] = acc[e, 0:3, :]


SMEM = pl.BlockSpec(memory_space=pltpu.SMEM)
HBM = pl.BlockSpec(memory_space=pltpu.HBM)
VMEM = pl.BlockSpec(memory_space=pltpu.VMEM)
PARAMS = pltpu.CompilerParams(vmem_limit_bytes=48 * 1024 * 1024)


def shape(*dims):
    return jax.ShapeDtypeStruct(dims, F32)


def gather_call(gp, ns, ds, pos, mass):
    return pl.pallas_call(
        gather_kernel,
        out_shape=(shape(NODE, 16, W), shape(64, W), shape(64, W)),
        in_specs=[HBM] * 5,
        out_specs=(VMEM,) * 3,
        scratch_shapes=[
            pltpu.SMEM(gp.shape, jnp.int32),
            pltpu.SMEM(ns.shape, jnp.int32),
            pltpu.SMEM(ds.shape, jnp.int32),
            pltpu.VMEM(pos.shape, F32),
            pltpu.VMEM(mass.shape, F32),
            pltpu.SMEM((32,), jnp.int32),
            pltpu.SMEM((REMOTE,), jnp.int32),
            pltpu.SemaphoreType.DMA((5,)),
        ],
        compiler_params=PARAMS,
    )(gp, ns, ds, pos, mass)


def local_call(pos, mass, metric):
    return pl.pallas_call(
        local_kernel,
        out_shape=(
            shape(9, NB, W),
            jax.ShapeDtypeStruct((NB, W, KDIM), BF),
            jax.ShapeDtypeStruct((NB, 32, W), BF),
        ),
        in_specs=[VMEM] * 3,
        out_specs=(VMEM,) * 3,
        scratch_shapes=[pltpu.VMEM((NB, KDIM, W), F32), pltpu.VMEM((NB, 32, W), F32)],
        compiler_params=PARAMS,
        cost_estimate=pl.CostEstimate(flops=10**9, bytes_accessed=10**6, transcendentals=0),
    )(pos, mass, metric)


def main_call(lp, gp, ns, ds, mass, energy, start_r, pt, fs, node_in, even_in, odd_in):
    return pl.pallas_call(
        main_kernel,
        out_shape=(
            shape(6, NB * W),
            shape(NB, W),
            shape(3, NB, W),
            shape(32, 4, W),
            shape(16, 4, W),
            shape(16, 4, W),
        ),
        in_specs=[SMEM] * 4 + [VMEM] * 8,
        out_specs=(VMEM,) * 6,
        scratch_shapes=[
            pltpu.SMEM((64,), jnp.int32),
            pltpu.SMEM((32,), jnp.int32),
            pltpu.VMEM((32, KDIM, W), F32),
            pltpu.VMEM((32, 32, W), F32),
            pltpu.VMEM((PARTS, W, KDIM), BF),
            pltpu.VMEM((PARTS, 32, W), BF),
            pltpu.VMEM((NB, KDIM, W), BF),
            pltpu.VMEM((NB, 16, W), F32),
            pltpu.VMEM((9, NB, W), F32),
            pltpu.VMEM((TILES, W, 2 * W), BF),
            pltpu.VMEM((NB, 32, W), BF),
            pltpu.VMEM((PARTS, 16, W), F32),
            pltpu.VMEM((3, NB, W), F32),
        ],
        compiler_params=PARAMS,
    )(lp, gp, ns, ds, mass, energy, start_r, pt, fs, node_in, even_in, odd_in)


def final_call(gp, ns, ds, acc, node_in, even_in, odd_in):
    return pl.pallas_call(
        final_kernel,
        out_shape=shape(3, NB * W),
        in_specs=[SMEM] * 3 + [VMEM] * 4,
        out_specs=VMEM,
        scratch_shapes=[
            pltpu.SMEM((32,), jnp.int32),
            pltpu.SMEM((REMOTE,), jnp.int32),
            pltpu.VMEM((NB, 4, W), F32),
        ],
        compiler_params=PARAMS,
    )(gp, ns, ds, acc, node_in, even_in, odd_in)


def exchange(node, even, odd, domains):
    def swaps(first):
        pairs = [(i, i + 1) for i in range(first, domains - 1, 2)]
        return pairs + [(b, a) for a, b in pairs]

    return (
        lax.all_to_all(node, "node", split_axis=0, concat_axis=0, tiled=True),
        lax.ppermute(even, "dom", swaps(0)),
        lax.ppermute(odd, "dom", swaps(1)),
    )


def on_device(
    domains, positions, masses, metric, energy, local_pairs, ghost_pairs, node_sends, domain_sends
):
    tables = (ghost_pairs, node_sends.transpose(0, 2, 1), domain_sends)
    mass = masses.reshape(NB, W)
    received = exchange(*gather_call(*tables, positions, mass), domains)
    prepared = local_call(positions, mass, metric)
    out_metric, density, acc, node, even, odd = main_call(
        local_pairs.transpose(1, 0), *tables, mass, energy.reshape(NB, W), *prepared, *received
    )
    returned = exchange(
        node.reshape(NODE, 16, W), even.reshape(64, W), odd.reshape(64, W), domains
    )
    acceleration = final_call(*tables, acc, *returned)
    return out_metric, density.reshape(-1), acceleration


def solution(mesh):
    both = ("dom", "node")
    in_specs = (
        P(None, both),
        P(both),
        P(None, both),
        P(both),
        P(both, None),
        P(both, None),
        P(both, None, None),
        P(both, None, None),
    )
    out_specs = (P(None, both), P(both), P(None, both))
    return jax.shard_map(
        functools.partial(on_device, mesh.shape["dom"]),
        mesh=mesh,
        in_specs=in_specs,
        out_specs=out_specs,
        check_vma=False,
    )
```

time: 73.7 us -> 53.3 us (0.72)
  Pallas kernels: 38 us -> 21.6 us
  starting transfers between devices: 28 us -> 24.7 us
    pallas_call x1, Pallas kernels: 34.2 us -> 18 us  [main_call(): pl.pallas_call(main_kernel, out_shape=(shape(6, NB * W), shape(NB, W), sh...]
    ppermute x4, starting transfers between devices: 18.2 us -> 15 us  [the longest x2 13 us: exchange(): lax.ppermute(odd, 'dom', swaps(1))]
    pallas_call x0 -> x1, Pallas kernels: none -> 0.75 us  [local_call(): pl.pallas_call(local_kernel, out_shape=(shape(9, NB, W), jax.ShapeDtypeSt...]
  transfers between devices with their start and end apart: 6 -> 6, of which waited for: 2 -> 2; matrix products, arithmetic and copies ran while one was open for 0% -> 0% of each run, Pallas kernels for 0% -> 1%
where the time goes in v1:
time: 53.3 us; the launch traced here: 52.8 us
  starting transfers between devices  24.7 us (46%)
  Pallas kernels  21.6 us (41%)
  waiting for transfers between devices  2.95 us (6%)
  local copies, waits for them, and re-layouts  2.8 us (5%)
  between operations  0.77 us (1%)
    pallas_call x1, Pallas kernels, main_call(): pl.pallas_call(main_kernel, out_shape=(shape(6, NB * W), shape(NB, W), sh...  18 us
    ppermute x2, starting transfers between devices, exchange(): lax.ppermute(odd, 'dom', swaps(1))  13 us
    all_to_all x2, starting transfers between devices, exchange(): lax.all_to_all(node, 'node', split_axis=0, concat_axis=0, tiled=True)  9.77 us
    ppermute x2, waiting for transfers between devices, exchange(): lax.ppermute(odd, 'dom', swaps(1))  2.94 us
    unnamed x20, local copies, waits for them, and re-layouts  2.8 us
    ppermute x2, starting transfers between devices, exchange(): lax.ppermute(even, 'dom', swaps(0))  1.92 us
    pallas_call x1, Pallas kernels, final_call(): pl.pallas_call(final_kernel, out_shape=shape(3, NB * W), in_specs=[SMEM]...  1.46 us
    pallas_call x1, Pallas kernels, gather_call(): pl.pallas_call(gather_kernel, out_shape=(shape(NODE, 16, W), shape(64, W)...  1.36 us
  transfers between devices with their start and end apart: 6, of which 2 were waited for; matrix products, arithmetic and copies ran while one was open for 0% of the time, Pallas kernels for 1%

profile of v1, /device:TPU:26, one launch (start us, length us, event | category | flops | bytes accessed | tf_op | source)
XLA Modules:
  0.0 52.8 jit_solution(10162167293907471095)
XLA Ops:
  0.6 0.0 copy-start.5
  0.6 0.0 copy-start.4
  0.7 0.0 copy-start.7
  0.7 0.7 %copy-done.5 = s32[1,2,8]{2,1,0:T(2,128)S(1)} copy-done((s32[1,2,8]{2,1,0:T(2,128)S(1)}, s32[1,2,8]{2,1,0:T(2,128)}, u32[]{:S(2)}) %copy-start.5) | copy-done | bytes 88
  1.3 0.0 copy-done.4
  1.3 0.0 copy-done.7
  1.3 0.7 %copy-done = f32[2048]{0:T(1024)S(1)} copy-done((f32[2048]{0:T(1024)S(1)}, f32[2048]{0:T(1024)}, u32[]{:S(2)}) %copy-start) | copy-done | bytes 8216
  2.0 0.8 %copy-done.2 = f32[3,2048]{1,0:T(4,128)S(1)} copy-done((f32[3,2048]{1,0:T(4,128)S(1)}, f32[3,2048]{1,0:T(4,128)}, u32[]{:S(2)}) %copy-start.2) | copy-done | bytes 24600
  2.8 1.4 %shard_map.104 = (f32[8,16,128]{2,1,0:T(8,128)}, f32[64,128]{1,0:T(8,128)S(1)}, f32[64,128]{1,0:T(8,128)S(1)}) custom-call(s32[1,32]{1,0:T(1,128)S(1)} %copy-done.7, s32[1,2,8]{2,1,0:T(2,128)S(1)} %bitcast.11, s32[1,2,8]{2,1,0:T(2,128)S(1)} %copy-done.5, f32[3,2048]{1,0:T(4,128)S(1)} %copy-done.2, f32[16,128]{1,0:T(8,128)S(1)} %bitcast.8), custom_call_target="tpu_custom_call" | custom-call | tf_op jit(solution)/shard_map/pallas_call | solution.py:413
  4.2 0.0 copy-start.1
  4.2 0.0 copy-start.3
  4.2 0.0 copy-start.9
  4.2 5.0 %all-to-all-start = ((f32[8,16,128]{2,1,0:T(8,128)}), f32[8,16,128]{2,1,0:T(8,128)S(1)}, u32[]{:S(2)}, u32[]{:S(2)}) async-start(f32[8,16,128]{2,1,0:T(8,128)} %get-tuple-element.18), calls=%async_computation | async-start | bytes 131072 | tf_op jit(solution)/shard_map/all_to_all | solution.py:501
  9.2 1.9 %collective-permute-start = (f32[64,128]{1,0:T(8,128)S(1)}, f32[64,128]{1,0:T(8,128)S(1)}, u32[]{:S(2)}, u32[]{:S(2)}) collective-permute-start(f32[64,128]{1,0:T(8,128)S(1)} %get-tuple-element.19), channel_id=1, source_target_pairs={{0,8},{16,24},{32,40},{48,56},{64,72},{80,88},{96,104},{112,120},{... | collective-permute-start | bytes 98312 | tf_op jit(solution)/shard_map/ppermute | solution.py:502
  11.1 7.0 %collective-permute-start.1 = (f32[64,128]{1,0:T(8,128)S(1)}, f32[64,128]{1,0:T(8,128)S(1)}, u32[]{:S(2)}, u32[]{:S(2)}) collective-permute-start(f32[64,128]{1,0:T(8,128)S(1)} %get-tuple-element.20), channel_id=1, source_target_pairs={{8,16},{24,32},{40,48},{56,64},{72,80},{88,96},{104,112},{120,128}... | collective-permute-start | bytes 98312 | tf_op jit(solution)/shard_map/ppermute | solution.py:503
  18.1 0.0 copy-done.1
  18.1 0.0 copy-done.3
  18.1 0.8 %shard_map.103 = (f32[9,16,128]{2,1,0:T(8,128)S(1)}, bf16[16,128,64]{2,1,0:T(8,128)(2,1)S(1)}, bf16[16,32,128]{2,1,0:T(8,128)(2,1)S(1)}) custom-call(f32[3,2048]{1,0:T(4,128)S(1)} %copy-done.3, f32[16,128]{1,0:T(8,128)S(1)} %bitcast.9, f32[6,2048]{1,0:T(8,128)S(1)} %copy-done.9), custom_call_target="tpu_custom_call" | custom-call | flops 1000000000 | bytes 1000000 | tf_op jit(solution)/shard_map/pallas_call | solution.py:433
  18.9 0.0 copy-start.6
  18.9 0.0 collective-permute-done.even_in
  18.9 1.1 %collective-permute-done.1.odd_in = f32[64,128]{1,0:T(8,128)S(1)} collective-permute-done((f32[64,128]{1,0:T(8,128)S(1)}, f32[64,128]{1,0:T(8,128)S(1)}, u32[]{:S(2)}, u32[]{:S(2)}) %collective-permute-start.1) | collective-permute-done | bytes 32800 | tf_op jit(solution)/shard_map/ppermute | solution.py:503
  20.0 0.0 all-to-all-done.node_in
  20.0 0.0 copy-done.6
  20.0 0.6 %copy-done.8 = s32[16,1]{0,1:T(1,128)S(1)} copy-done((s32[16,1]{0,1:T(1,128)S(1)}, s32[16,1]{0,1:T(1,128)}, u32[]{:S(2)}) %copy-start.8) | copy-done | bytes 88
  20.7 18.0 %shard_map.105 = (f32[6,2048]{1,0:T(8,128)}, f32[16,128]{1,0:T(8,128)}, f32[3,16,128]{2,1,0:T(8,128)S(1)}, f32[32,4,128]{2,1,0:T(4,128)}, f32[16,4,128]{2,1,0:T(4,128)S(1)}, /*index=5*/f32[16,4,128]{2,1,0:T(4,128)S(1)}) custom-call(s32[1,16]{1,0:T(1,128)S(1)} %bitcast.15, s32[1,32]{1,0:T(1,128)S(1)} %copy-done.7, s32[1,2,8]{2,1,0:T(2,128)S(1)} %bitcast.12, ...), custom_call_target="tpu_custom_call" | custom-call | tf_op jit(solution)/shard_map/pallas_call | solution.py:449
  38.6 4.8 %all-to-all-start.1 = ((f32[8,16,128]{2,1,0:T(8,128)}), f32[8,16,128]{2,1,0:T(8,128)S(1)}, u32[]{:S(2)}, u32[]{:S(2)}) async-start(f32[8,16,128]{2,1,0:T(8,128)} %bitcast.5), calls=%async_computation.1 | async-start | bytes 131072 | tf_op jit(solution)/shard_map/all_to_all | solution.py:501
  43.4 0.0 collective-permute-start.2
  43.4 6.0 %collective-permute-start.3 = (f32[64,128]{1,0:T(8,128)S(1)}, f32[64,128]{1,0:T(8,128)S(1)}, u32[]{:S(2)}, u32[]{:S(2)}) collective-permute-start(f32[64,128]{1,0:T(8,128)S(1)} %bitcast.16), channel_id=1, source_target_pairs={{8,16},{24,32},{40,48},{56,64},{72,80},{88,96},{104,112},{120,128}... | collective-permute-start | bytes 98312 | tf_op jit(solution)/shard_map/ppermute | solution.py:503
  49.5 0.0 collective-permute-done.2.even_in
  49.5 1.9 %collective-permute-done.3.odd_in = f32[64,128]{1,0:T(8,128)S(1)} collective-permute-done((f32[64,128]{1,0:T(8,128)S(1)}, f32[64,128]{1,0:T(8,128)S(1)}, u32[]{:S(2)}, u32[]{:S(2)}) %collective-permute-start.3) | collective-permute-done | bytes 32800 | tf_op jit(solution)/shard_map/ppermute | solution.py:503
  51.3 0.0 all-to-all-done.1.node_in
  51.3 1.5 %shard_map.106 = f32[3,2048]{1,0:T(4,128)} custom-call(s32[1,32]{1,0:T(1,128)S(1)} %copy-done.7, s32[1,2,8]{2,1,0:T(2,128)S(1)} %bitcast.13, s32[1,2,8]{2,1,0:T(2,128)S(1)} %copy-done.5, f32[3,16,128]{2,1,0:T(8,128)S(1)} %get-tuple-element.23.acc_in, f32[8,16,128]{2,1,0:T(8,128)S(1)} %all-to-all-done.1.node_in, ...), custom_call_target="tpu_custom_call" | custom-call | tf_op jit(solution)/shard_map/pallas_call | solution.py:481
  (4 shorter events, 0.0 us)
Async XLA Ops:
  0.6 0.7 %copy-start.5 = (s32[1,2,8]{2,1,0:T(2,128)S(1)}, s32[1,2,8]{2,1,0:T(2,128)}, u32[]{:S(2)}) copy-start(s32[1,2,8]{2,1,0:T(2,128)} %ds.3) | copy-start | bytes 196
  0.6 0.7 %copy-start.4 = (s32[1,8,2]{1,2,0:T(2,128)S(1)}, s32[1,8,2]{1,2,0:T(2,128)}, u32[]{:S(2)}) copy-start(s32[1,8,2]{1,2,0:T(2,128)} %param.14) | copy-start | bytes 196
  0.7 0.7 %copy-start.7 = (s32[1,32]{1,0:T(1,128)S(1)}, s32[1,32]{1,0:T(1,128)}, u32[]{:S(2)}) copy-start(s32[1,32]{1,0:T(1,128)} %gp.3) | copy-start | bytes 388
  1.3 0.7 %copy-start = (f32[2048]{0:T(1024)S(1)}, f32[2048]{0:T(1024)}, u32[]{:S(2)}) copy-start(f32[2048]{0:T(1024)} %param.9) | copy-start | bytes 24580
  2.0 0.8 %copy-start.2 = (f32[3,2048]{1,0:T(4,128)S(1)}, f32[3,2048]{1,0:T(4,128)}, u32[]{:S(2)}) copy-start(f32[3,2048]{1,0:T(4,128)} %pos_in.1) | copy-start | bytes 73732
  4.2 14.0 %copy-start.1 = (f32[2048]{0:T(1024)S(1)}, f32[2048]{0:T(1024)}, u32[]{:S(2)}) copy-start(f32[2048]{0:T(1024)} %param.9) | copy-start | bytes 24580
  4.2 14.0 %copy-start.3 = (f32[3,2048]{1,0:T(4,128)S(1)}, f32[3,2048]{1,0:T(4,128)}, u32[]{:S(2)}) copy-start(f32[3,2048]{1,0:T(4,128)} %pos_in.1) | copy-start | bytes 73732
  4.2 14.0 %copy-start.9 = (f32[6,2048]{1,0:T(8,128)S(1)}, f32[6,2048]{1,0:T(8,128)}, u32[]{:S(2)}) copy-start(f32[6,2048]{1,0:T(8,128)} %metric.1) | copy-start | bytes 147460
  4.2 15.8 %all-to-all-start = ((f32[8,16,128]{2,1,0:T(8,128)}), f32[8,16,128]{2,1,0:T(8,128)S(1)}, u32[]{:S(2)}, u32[]{:S(2)}) async-start(f32[8,16,128]{2,1,0:T(8,128)} %get-tuple-element.18), calls=%async_computation | async-start | bytes 131072 | tf_op jit(solution)/shard_map/all_to_all | solution.py:501
  9.2 9.8 %collective-permute-start = (f32[64,128]{1,0:T(8,128)S(1)}, f32[64,128]{1,0:T(8,128)S(1)}, u32[]{:S(2)}, u32[]{:S(2)}) collective-permute-start(f32[64,128]{1,0:T(8,128)S(1)} %get-tuple-element.19), channel_id=1, source_target_pairs={{0,8},{16,24},{32,40},{48,56},{64,72},{80,88},{96,104},{112,120},{... | collective-permute-start | bytes 98312 | tf_op jit(solution)/shard_map/ppermute | solution.py:502
  11.1 8.9 %collective-permute-start.1 = (f32[64,128]{1,0:T(8,128)S(1)}, f32[64,128]{1,0:T(8,128)S(1)}, u32[]{:S(2)}, u32[]{:S(2)}) collective-permute-start(f32[64,128]{1,0:T(8,128)S(1)} %get-tuple-element.20), channel_id=1, source_target_pairs={{8,16},{24,32},{40,48},{56,64},{72,80},{88,96},{104,112},{120,128}... | collective-permute-start | bytes 98312 | tf_op jit(solution)/shard_map/ppermute | solution.py:503
  18.9 1.1 %copy-start.6 = (f32[2048]{0:T(1024)S(1)}, f32[2048]{0:T(1024)}, u32[]{:S(2)}) copy-start(f32[2048]{0:T(1024)} %param.11) | copy-start | bytes 24580
  20.0 0.7 %copy-start.8 = (s32[16,1]{0,1:T(1,128)S(1)}, s32[16,1]{0,1:T(1,128)}, u32[]{:S(2)}) copy-start(s32[16,1]{0,1:T(1,128)} %param.12) | copy-start | bytes 196
  38.6 12.7 %all-to-all-start.1 = ((f32[8,16,128]{2,1,0:T(8,128)}), f32[8,16,128]{2,1,0:T(8,128)S(1)}, u32[]{:S(2)}, u32[]{:S(2)}) async-start(f32[8,16,128]{2,1,0:T(8,128)} %bitcast.5), calls=%async_computation.1 | async-start | bytes 131072 | tf_op jit(solution)/shard_map/all_to_all | solution.py:501
  43.4 6.0 %collective-permute-start.2 = (f32[64,128]{1,0:T(8,128)S(1)}, f32[64,128]{1,0:T(8,128)S(1)}, u32[]{:S(2)}, u32[]{:S(2)}) collective-permute-start(f32[64,128]{1,0:T(8,128)S(1)} %bitcast.17), channel_id=1, source_target_pairs={{0,8},{16,24},{32,40},{48,56},{64,72},{80,88},{96,104},{112,120},{... | collective-permute-start | bytes 98312 | tf_op jit(solution)/shard_map/ppermute | solution.py:502
  43.4 7.9 %collective-permute-start.3 = (f32[64,128]{1,0:T(8,128)S(1)}, f32[64,128]{1,0:T(8,128)S(1)}, u32[]{:S(2)}, u32[]{:S(2)}) collective-permute-start(f32[64,128]{1,0:T(8,128)S(1)} %bitcast.16), channel_id=1, source_target_pairs={{8,16},{24,32},{40,48},{56,64},{72,80},{88,96},{104,112},{120,128}... | collective-permute-start | bytes 98312 | tf_op jit(solution)/shard_map/ppermute | solution.py:503

commit v2 on v1

v2 whole, which is shorter than its diff:
```python
import functools

import jax
import jax.numpy as jnp
from jax import lax
from jax.experimental import pallas as pl
from jax.experimental.pallas import tpu as pltpu
from jax.sharding import PartitionSpec as P

W = 128
NB = 16
HALF = NB // 2
ITERS = 3
NODE = 8
REMOTE = 64
PARTS = NB + REMOTE
TILES = 96
KDIM = 64
ADIABATIC = 5.0 / 3.0
TARGET_SCALE = 0.5
RIDGE_TERM = 0.1
BF = jnp.bfloat16
F32 = jnp.float32


def side_of(pairing):
    return lax.rem(lax.axis_index("dom") + pairing + 1, 2)


def split2(value):
    high = value.astype(BF)
    rest = value - high.astype(F32)
    return high, rest.astype(BF)


def split3(value):
    high = value.astype(BF).astype(F32)
    rest = value - high
    middle = rest.astype(BF).astype(F32)
    return high, middle, rest - middle


def send_tables(gp, ns, ds, inv, sent):
    for slot in range(32):
        inv[gp[0, slot]] = slot // 2
    for s in range(NODE):
        for k in range(2):
            sent[4 * s + k] = ns[0, k, s]
            sent[4 * s + 2 + k] = inv[2 * s + k]
    for pairing in range(2):
        side = side_of(pairing)
        for k in range(8):
            sent[32 + 16 * pairing + k] = ds[0, side, k]
            sent[40 + 16 * pairing + k] = inv[16 + 8 * side + k]


def lanes(block):
    return pl.ds(pl.multiple_of(block * W, W), W)


def gather_kernel(
    gp_in, ns_in, ds_in, pos_in, mass_in, node_out, even_out, odd_out, sent,
    gp, ns, ds, pos, mass, inv, sems,
):
    pairs = ((gp_in, gp), (ns_in, ns), (ds_in, ds), (pos_in, pos), (mass_in, mass))
    copies = [
        pltpu.make_async_copy(source, target, sems.at[c])
        for c, (source, target) in enumerate(pairs)
    ]
    for copy in copies:
        copy.start()
    for copy in copies:
        copy.wait()
    send_tables(gp, ns, ds, inv, sent)
    for t in range(REMOTE):
        b = sent[t]
        place, weight = pos[:, lanes(b)], mass[pl.ds(b, 1), :]
        out = node_out.at[t // 4] if t < 32 else (even_out if t < 48 else odd_out)
        row = 4 * (t % 4) if t < 32 else 4 * (t % 16)
        out[row : row + 3, :] = place
        out[row + 3 : row + 4, :] = weight


def inverse_parts(m):
    cofactors = (
        m[1] * m[2] - m[5] * m[5],
        m[0] * m[2] - m[4] * m[4],
        m[0] * m[1] - m[3] * m[3],
        m[4] * m[5] - m[3] * m[2],
        m[3] * m[5] - m[4] * m[1],
        m[3] * m[4] - m[0] * m[5],
    )
    return cofactors, m[0] * cofactors[0] + m[3] * cofactors[3] + m[4] * cofactors[4]


def apply_metric(g, r):
    return (
        g[0] * r[0] + g[3] * r[1] + g[4] * r[2],
        g[3] * r[0] + g[1] * r[1] + g[5] * r[2],
        g[4] * r[0] + g[5] * r[1] + g[2] * r[2],
    )


def products(r):
    return (
        r[0] * r[0],
        r[1] * r[1],
        r[2] * r[2],
        r[0] * r[1],
        r[0] * r[2],
        r[1] * r[2],
    )


def reciprocal(value):
    guess = pl.reciprocal(value, approx=True)
    return guess * (2.0 - value * guess)


def unit_kernel(unit):
    rows = lax.broadcasted_iota(jnp.int32, (W, W), 0)
    unit[...] = (rows == lax.broadcasted_iota(jnp.int32, (W, W), 1)).astype(F32).astype(BF)


def spread(unit, stage, feat, pt, fs, first, place, weight):
    n = place[0].shape[0]
    values = list(place) + list(products(place))
    for f, value in enumerate(values):
        high, middle, low = split3(value)
        for row, piece in zip((0, 9, 18, 27, 36, 45), (high, high, middle, high, middle, low)):
            stage[0:n, row + f, :] = piece
    for row in (54, 55, 56):
        stage[0:n, row, :] = jnp.ones((n, W), F32)
    for row in range(57, KDIM):
        stage[0:n, row, :] = jnp.zeros((n, W), F32)
    for f, value in enumerate([weight] + [weight * v for v in values]):
        high = value.astype(BF).astype(F32)
        feat[0:n, f, :] = high
        feat[0:n, 16 + f, :] = value - high
    for f in range(10, 16):
        feat[0:n, f, :] = jnp.zeros((n, W), F32)
        feat[0:n, 16 + f, :] = jnp.zeros((n, W), F32)
    for b in range(n):
        if b % 2:
            pt[first + b] = jnp.transpose(stage[b]).astype(BF)
        else:
            turned = lax.dot_general(
                unit, stage[b].astype(BF), (((1,), (1,)), ((), ())), preferred_element_type=F32
            )
            pt[first + b] = turned.astype(BF)
        fs[first + b] = feat[b].astype(BF)


def form_coefficients(g, r):
    gr = apply_metric(g, r)
    constant = 1.0 + r[0] * gr[0] + r[1] * gr[1] + r[2] * gr[2]
    return [constant] + [-2.0 * v for v in gr] + list(g[0:3]) + [2.0 * v for v in g[3:6]]


def build_q(stage, q, half, g, r):
    constant, *others = form_coefficients(g, r)
    n = HALF
    for f, value in enumerate(others):
        high, middle, low = split3(value)
        for row, piece in zip((0, 9, 18, 27, 36, 45), (high, middle, high, low, middle, high)):
            stage[half, :, row + f, :] = piece
    for row, piece in zip((54, 55, 56), split3(constant)):
        stage[half, :, row, :] = piece
    for row in range(57, KDIM):
        stage[half, :, row, :] = jnp.zeros((n, W), F32)
    for e in range(n):
        q[n * half + e] = stage[half, e].astype(BF)


def rows_of(half):
    return slice(HALF * half, HALF * half + HALF)


def contract(features, high, middle):
    both = jnp.concatenate([features, features], axis=1)
    out = jnp.dot(both, jnp.concatenate([high, middle], axis=0), preferred_element_type=F32)
    return out[0:16] + out[16:32]


def variable_partner(t):
    if t < 16:
        return t
    return 56 + (t - 16) if t < 24 else 72 + (t - 24)


def local_kernel(unit, pos, mass, metric, own_r, pt, fs, q, stage, feat, stage_q):
    for e in range(NB):
        own_r[0:3, e, :] = pos[:, e * W : (e + 1) * W]
        own_r[3:9, e, :] = metric[:, e * W : (e + 1) * W]
    for half in range(2):
        rows = rows_of(half)
        g = [own_r[3 + c, rows, :] for c in range(6)]
        build_q(stage_q, q, half, g, [own_r[c, rows, :] for c in range(3)])
    spread(unit[...], stage, feat, pt, fs, 0, [own_r[c] for c in range(3)], mass[...])


def turn_back(features, weights):
    both = jnp.concatenate([features, features], axis=1)
    out = lax.dot_general(both, weights, (((1,), (1,)), ((), ())), preferred_element_type=F32)
    return out[0:16] + out[16:32]


def push(back, first, count, place):
    b = [back[first : first + count, f, :] for f in range(9)]
    moved = apply_metric(b, place)
    return [moved[c] - b[6 + c] for c in range(3)]


def main_kernel(
    lp,
    gp,
    ns,
    ds,
    mass,
    energy,
    start_r,
    pt_local,
    fs_local,
    q_start,
    node_in,
    even_in,
    odd_in,
    node_out,
    even_out,
    odd_out,
    own_r,
    h,
    w3_local,
    part,
    own,
    stage,
    feat,
    pt,
    fs,
    q,
    stage_q,
    feat_h,
    sums,
    w3,
    back,
):
    for e in range(NB):
        part[4 * e] = lp[0, e]
        own[e] = lp[0, e]
        for k in range(2):
            g = gp[0, 2 * e + k]
            pairing = side_of(g // 8)
            part[4 * e + 1 + k] = jnp.where(
                g < 16, 16 + (g // 2) * 4 + g % 2, 48 + 16 * pairing + g % 8
            )
    for s in range(NODE):
        for k in range(2):
            part[4 * ns[0, k, s] + 3] = 16 + 4 * s + 2 + k
            own[16 + 8 * k + s] = ds[0, side_of(k), s]
    own_r[0:9] = start_r[...]
    pt[0:NB] = pt_local[...]
    fs[0:NB] = fs_local[...]
    q[...] = q_start[...]
    node_view = node_in[...].reshape(32, 4, W)
    even_view = even_in[...].reshape(16, 4, W)
    odd_view = odd_in[...].reshape(16, 4, W)
    rows = lax.broadcasted_iota(jnp.int32, (W, W), 0)
    eye = (rows == lax.broadcasted_iota(jnp.int32, (W, W), 1)).astype(F32).astype(BF)
    for base, view in ((16, node_view), (48, even_view), (64, odd_view)):
        at = pl.ds(base - NB, view.shape[0])
        spread(
            eye, stage.at[at], feat.at[at], pt, fs, base, [view[:, c, :] for c in range(3)], view[:, 3, :]
        )

    def place_of(half):
        return [own_r[c, rows_of(half), :] for c in range(3)]

    def metric_of(half):
        return [own_r[3 + c, rows_of(half), :] for c in range(6)]

    def fixed_tiles(half, body):
        for e in range(HALF * half, HALF * half + HALF):
            partners = [part[4 * e + c] for c in range(4)]
            rows = jnp.concatenate([pt[p] for p in partners], axis=0)
            s = jnp.dot(rows, q[e], preferred_element_type=F32)
            features = jnp.concatenate([fs[p] for p in partners], axis=1)
            out = body(e, s, features)
            if half == 0:
                sums[e] = out
            else:
                sums[e] = sums[e] + out

    def variable_tiles(body):
        sums[rows_of(1)] = jnp.zeros((HALF, 16, W), F32)
        for t in range(32):
            p = variable_partner(t)
            e = own[t]
            s = jnp.dot(pt[p], q[e], preferred_element_type=F32)
            sums[e] = sums[e] + body(t, s, fs[p])

    def moments(_, s, features):
        weight = reciprocal(s * s)
        return contract(features, *split2(weight))

    def next_metric(half):
        r, g = place_of(half), metric_of(half)
        m = [sums[rows_of(half), f, :] for f in range(10)]
        total = m[0]

        def second(a, b, joint):
            return (
                r[a] * r[b] * total - r[a] * m[1 + b] - r[b] * m[1 + a] + m[joint]
            ) / total

        spread_now = [
            second(0, 0, 4) + RIDGE_TERM,
            second(1, 1, 5) + RIDGE_TERM,
            second(2, 2, 6) + RIDGE_TERM,
            second(0, 1, 7),
            second(0, 2, 8),
            second(1, 2, 9),
        ]
        cofactors, determinant = inverse_parts(spread_now)
        g = [0.5 * g[c] + 0.5 * TARGET_SCALE * cofactors[c] / determinant for c in range(6)]
        for c in range(6):
            own_r[3 + c, rows_of(half), :] = g[c]
        build_q(stage_q, q, half, g, r)

    def iteration(_, carry):
        fixed_tiles(0, moments)
        variable_tiles(moments)
        fixed_tiles(1, moments)
        next_metric(0)
        next_metric(1)
        return carry

    lax.fori_loop(0, ITERS, iteration, 0)

    def cubes(s):
        inverse = reciprocal(s)
        return split2(inverse * inverse * inverse)

    def keep(ref, row, high3, middle3):
        ref[row, :, 0:W] = high3
        ref[row, :, W:] = middle3

    def final_fixed(e, s, features):
        high3, middle3 = cubes(s)
        for c in range(4):
            ref, row = (w3_local, e) if c == 0 else (w3, 3 * e + c - 1)
            keep(ref, row, high3[c * W : (c + 1) * W], middle3[c * W : (c + 1) * W])
        return contract(features, high3, middle3)

    def final_variable(t, s, features):
        high3, middle3 = cubes(s)
        keep(*((w3_local, 16 + t) if t < 16 else (w3, 32 + t)), high3, middle3)
        return contract(features, high3, middle3)

    def finish(half):
        rows = rows_of(half)
        r, g = place_of(half), metric_of(half)
        _, determinant = inverse_parts(g)
        volume = jnp.sqrt(determinant) / 384.0
        m = [sums[rows, f, :] for f in range(10)]
        density_sum = 0.0
        for coefficient, value in zip(form_coefficients(g, r), m):
            density_sum = density_sum + coefficient * value
        density = volume * density_sum
        own_r[12, rows, :] = density
        coefficient = (ADIABATIC - 1.0) * energy[rows, :] / density * volume
        scale = 4.0 * coefficient
        pull = apply_metric(g, [r[c] * m[0] - m[1 + c] for c in range(3)])
        for c in range(3):
            own_r[9 + c, rows, :] = scale * pull[c]
        scale = scale * mass[rows, :]
        for f, value in enumerate(list(g) + list(apply_metric(g, r))):
            value = scale * value
            high = value.astype(BF).astype(F32)
            feat_h[rows, f, :] = high
            feat_h[rows, 16 + f, :] = value - high
        for f in list(range(9, 16)) + list(range(25, 32)):
            feat_h[rows, f, :] = jnp.zeros((HALF, W), F32)
        for e in range(HALF * half, HALF * half + HALF):
            h[e] = feat_h[e].astype(BF)

    fixed_tiles(0, final_fixed)
    variable_tiles(final_variable)
    fixed_tiles(1, final_fixed)
    finish(0)
    finish(1)

    for t in range(16, 32):
        back[variable_partner(t) - NB] = turn_back(h[own[t]], w3[32 + t])
    for e in range(NB):
        for c in range(1, 4):
            back[part[4 * e + c] - NB] = turn_back(h[e], w3[3 * e + c - 1])
    for first, count, view, out in (
        (0, 32, node_view, node_out),
        (32, 16, even_view, even_out),
        (48, 16, odd_view, odd_out),
    ):
        place = [view[:, c, :] for c in range(3)]
        values = push(back, first, count, place)
        for c in range(3):
            out[:, c, :] = values[c]
        out[:, 3, :] = jnp.zeros((count, W), F32)


def rest_kernel(lp, own_r, h, w3_local, acc_out, back):
    for t in range(16):
        back[t] = turn_back(h[lp[0, t]], w3_local[16 + t])
    for e in range(NB):
        p = lp[0, e]
        back[p] = back[p] + turn_back(h[e], w3_local[e])
    local = push(back, 0, NB, [own_r[c] for c in range(3)])
    for c in range(3):
        acc_out[:, c, :] = own_r[9 + c] + local[c]
    acc_out[:, 3, :] = jnp.zeros((NB, W), F32)


def final_kernel(
    sent, own_r, acc_in, node_in, even_in, odd_in, metric_out, density_out, out,
    acc, metric, flat, sems,
):
    for e in range(NB):
        metric[:, e * W : (e + 1) * W] = own_r[3:9, e, :]
    copies = [
        pltpu.make_async_copy(metric, metric_out, sems.at[0]),
        pltpu.make_async_copy(own_r.at[12], density_out, sems.at[1]),
        pltpu.make_async_copy(flat, out, sems.at[2]),
    ]
    copies[0].start()
    copies[1].start()
    acc[...] = acc_in[...]
    for t in range(REMOTE):
        b = sent[t]
        if t < 32:
            value = node_in[t // 4, 4 * (t % 4) : 4 * (t % 4) + 4, :]
        else:
            value = (even_in if t < 48 else odd_in)[4 * (t % 16) : 4 * (t % 16) + 4, :]
        acc[b] = acc[b] + value
    for e in range(NB):
        flat[:, e * W : (e + 1) * W] = acc[e, 0:3, :]
    copies[2].start()
    for copy in copies:
        copy.wait()


SMEM = pl.BlockSpec(memory_space=pltpu.SMEM)
HBM = pl.BlockSpec(memory_space=pltpu.HBM)
VMEM = pl.BlockSpec(memory_space=pltpu.VMEM)
PARAMS = pltpu.CompilerParams(vmem_limit_bytes=48 * 1024 * 1024)


def shape(*dims):
    return jax.ShapeDtypeStruct(dims, F32)


def narrow(*dims):
    return jax.ShapeDtypeStruct(dims, BF)


def table(*dims):
    return jax.ShapeDtypeStruct(dims, jnp.int32)


BESIDE = pl.CostEstimate(flops=10**9, bytes_accessed=10**6, transcendentals=0)


def gather_call(gp, ns, ds, pos, mass):
    return pl.pallas_call(
        gather_kernel,
        out_shape=(shape(NODE, 16, W), shape(64, W), shape(64, W), table(REMOTE)),
        in_specs=[HBM] * 5,
        out_specs=(VMEM, VMEM, VMEM, SMEM),
        scratch_shapes=[
            pltpu.SMEM(gp.shape, jnp.int32),
            pltpu.SMEM(ns.shape, jnp.int32),
            pltpu.SMEM(ds.shape, jnp.int32),
            pltpu.VMEM(pos.shape, F32),
            pltpu.VMEM(mass.shape, F32),
            pltpu.SMEM((32,), jnp.int32),
            pltpu.SemaphoreType.DMA((5,)),
        ],
        compiler_params=pltpu.CompilerParams(vmem_limit_bytes=64 * 2**20),
    )(gp, ns, ds, pos, mass)


def local_call(unit, pos, mass, metric):
    return pl.pallas_call(
        local_kernel,
        out_shape=(
            shape(9, NB, W),
            narrow(NB, W, KDIM),
            narrow(NB, 32, W),
            narrow(NB, KDIM, W),
        ),
        in_specs=[VMEM] * 4,
        out_specs=(VMEM,) * 4,
        scratch_shapes=[
            pltpu.VMEM((NB, KDIM, W), F32),
            pltpu.VMEM((NB, 32, W), F32),
            pltpu.VMEM((2, HALF, KDIM, W), F32),
        ],
        compiler_params=pltpu.CompilerParams(vmem_limit_bytes=8 * 2**20),
        cost_estimate=BESIDE,
    )(unit, pos, mass, metric)


def unit_call():
    return pl.pallas_call(
        unit_kernel,
        out_shape=narrow(W, W),
        out_specs=VMEM,
        compiler_params=pltpu.CompilerParams(vmem_limit_bytes=8 * 2**20),
        cost_estimate=BESIDE,
    )()


def main_call(lp, gp, ns, ds, mass, energy, start_r, pt, fs, q, node_in, even_in, odd_in):
    return pl.pallas_call(
        main_kernel,
        out_shape=(
            shape(32, 4, W),
            shape(16, 4, W),
            shape(16, 4, W),
            shape(13, NB, W),
            narrow(NB, 32, W),
            narrow(32, W, 2 * W),
        ),
        in_specs=[SMEM] * 4 + [VMEM] * 9,
        out_specs=(VMEM,) * 6,
        scratch_shapes=[
            pltpu.SMEM((64,), jnp.int32),
            pltpu.SMEM((32,), jnp.int32),
            pltpu.VMEM((REMOTE, KDIM, W), F32),
            pltpu.VMEM((REMOTE, 32, W), F32),
            pltpu.VMEM((PARTS, W, KDIM), BF),
            pltpu.VMEM((PARTS, 32, W), BF),
            pltpu.VMEM((NB, KDIM, W), BF),
            pltpu.VMEM((2, HALF, KDIM, W), F32),
            pltpu.VMEM((NB, 32, W), F32),
            pltpu.VMEM((NB, 16, W), F32),
            pltpu.VMEM((REMOTE, W, 2 * W), BF),
            pltpu.VMEM((REMOTE, 16, W), F32),
        ],
        compiler_params=pltpu.CompilerParams(vmem_limit_bytes=32 * 2**20),
    )(lp, gp, ns, ds, mass, energy, start_r, pt, fs, q, node_in, even_in, odd_in)


def rest_call(lp, own_r, h, w3_local):
    return pl.pallas_call(
        rest_kernel,
        out_shape=shape(NB, 4, W),
        in_specs=[SMEM] + [VMEM] * 3,
        out_specs=VMEM,
        scratch_shapes=[pltpu.VMEM((NB, 16, W), F32)],
        compiler_params=pltpu.CompilerParams(vmem_limit_bytes=8 * 2**20),
        cost_estimate=BESIDE,
    )(lp, own_r, h, w3_local)


def final_call(sent, own_r, acc, node_in, even_in, odd_in):
    return pl.pallas_call(
        final_kernel,
        out_shape=(shape(6, NB * W), shape(NB, W), shape(3, NB * W)),
        in_specs=[SMEM] + [VMEM] * 5,
        out_specs=(HBM,) * 3,
        scratch_shapes=[
            pltpu.VMEM((NB, 4, W), F32),
            pltpu.VMEM((6, NB * W), F32),
            pltpu.VMEM((3, NB * W), F32),
            pltpu.SemaphoreType.DMA((3,)),
        ],
        compiler_params=pltpu.CompilerParams(vmem_limit_bytes=8 * 2**20),
    )(sent, own_r, acc, node_in, even_in, odd_in)


def exchange(node, even, odd, domains):
    def swaps(first):
        pairs = [(i, i + 1) for i in range(first, domains - 1, 2)]
        return pairs + [(b, a) for a, b in pairs]

    return (
        lax.all_to_all(node, "node", split_axis=0, concat_axis=0, tiled=True),
        lax.ppermute(even, "dom", swaps(0)),
        lax.ppermute(odd, "dom", swaps(1)),
    )


def on_device(
    domains, positions, masses, metric, energy, local_pairs, ghost_pairs, node_sends, domain_sends
):
    tables = (ghost_pairs, node_sends.transpose(0, 2, 1), domain_sends)
    mass = masses.reshape(NB, W)
    *sends, sent = gather_call(*tables, positions, mass)
    received = exchange(*sends, domains)
    lp = local_pairs.transpose(1, 0)
    unit = unit_call()
    start_r, pt, fs, q = local_call(unit, positions, mass, metric)
    node, even, odd, own_r, h, w3_local = main_call(
        lp, *tables, mass, energy.reshape(NB, W), start_r, pt, fs, q, *received
    )
    returned = exchange(
        node.reshape(NODE, 16, W), even.reshape(64, W), odd.reshape(64, W), domains
    )
    acc = rest_call(lp, own_r, h, w3_local)
    out_metric, density, acceleration = final_call(sent, own_r, acc, *returned)
    return out_metric, density.reshape(-1), acceleration


def solution(mesh):
    both = ("dom", "node")
    in_specs = (
        P(None, both),
        P(both),
        P(None, both),
        P(both),
        P(both, None),
        P(both, None),
        P(both, None, None),
        P(both, None, None),
    )
    out_specs = (P(None, both), P(both), P(None, both))
    return jax.shard_map(
        functools.partial(on_device, mesh.shape["dom"]),
        mesh=mesh,
        in_specs=in_specs,
        out_specs=out_specs,
        check_vma=False,
    )
```

time: 53.3 us -> 48.8 us (0.916)
  local copies, waits for them, and re-layouts: 2.8 us -> 0.05 us
  waiting for transfers between devices: 2.95 us -> 1.35 us
    unnamed x20 -> x18, local copies, waits for them, and re-layouts: 2.8 us -> 0.05 us
    ppermute x2, waiting for transfers between devices: 2.94 us -> 1.34 us  [exchange(): lax.ppermute(odd, 'dom', swaps(1))]
    pallas_call x3 -> x5, Pallas kernels: 20.2 us -> 19.8 us  [the longest x1 15.8 us: main_call(): pl.pallas_call(main_kernel, out_shape=(shape(32, 4, W), shape(16, 4, W),...]
  transfers between devices with their start and end apart: 6 -> 6, of which waited for: 2 -> 2; matrix products, arithmetic and copies ran while one was open for 0% -> 0% of each run, Pallas kernels for 1% -> 5%
where the time goes in v2:
time: 48.8 us; the launch traced here: 48.5 us
  starting transfers between devices  24.9 us (51%)
  Pallas kernels  21.4 us (44%)
  waiting for transfers between devices  1.35 us (3%)
  between operations  0.81 us (2%)
    pallas_call x1, Pallas kernels, main_call(): pl.pallas_call(main_kernel, out_shape=(shape(32, 4, W), shape(16, 4, W),...  15.8 us
    ppermute x2, starting transfers between devices, exchange(): lax.ppermute(odd, 'dom', swaps(1))  13.1 us
    all_to_all x2, starting transfers between devices, exchange(): lax.all_to_all(node, 'node', split_axis=0, concat_axis=0, tiled=True)  9.9 us
    ppermute x2, starting transfers between devices, exchange(): lax.ppermute(even, 'dom', swaps(0))  1.92 us
    pallas_call x1, Pallas kernels, gather_call(): pl.pallas_call(gather_kernel, out_shape=(shape(NODE, 16, W), shape(64, W)...  1.6 us
    pallas_call x1, Pallas kernels, final_call(): pl.pallas_call(final_kernel, out_shape=(shape(6, NB * W), shape(NB, W), s...  1.45 us
    pallas_call x1, Pallas kernels, rest_call(): pl.pallas_call(rest_kernel, out_shape=shape(NB, 4, W), in_specs=[SMEM] +...  1.4 us
    ppermute x2, waiting for transfers between devices, exchange(): lax.ppermute(odd, 'dom', swaps(1))  1.34 us
  transfers between devices with their start and end apart: 6, of which 2 were waited for; matrix products, arithmetic and copies ran while one was open for 0% of the time, Pallas kernels for 5%

profile of v2, /device:TPU:26, one launch (start us, length us, event | category | flops | bytes accessed | tf_op | source)
XLA Modules:
  0.0 48.5 jit_solution(11495889588410527375)
XLA Ops:
  0.6 1.6 %shard_map.103 = (f32[8,16,128]{2,1,0:T(8,128)}, f32[64,128]{1,0:T(8,128)}, f32[64,128]{1,0:T(8,128)}, s32[64]{0:T(128)}) custom-call(s32[1,32]{1,0:T(1,128)} %gp.1, s32[1,2,8]{2,1,0:T(2,128)} %bitcast.12, s32[1,2,8]{2,1,0:T(2,128)} %ds.1, f32[3,2048]{1,0:T(4,128)} %pos.1, f32[16,128]{1,0:T(8,128)} %bitcast.8), custom_call_target="tpu_custom_call" | custom-call | tf_op jit(solution)/shard_map/pallas_call | solution.py:471
  2.2 0.0 copy-start
  2.2 0.0 copy-start.1
  2.3 0.0 copy-start.8
  2.3 5.0 %all-to-all-start = ((f32[8,16,128]{2,1,0:T(8,128)}), f32[8,16,128]{2,1,0:T(8,128)S(1)}, u32[]{:S(2)}, u32[]{:S(2)}) async-start(f32[8,16,128]{2,1,0:T(8,128)} %get-tuple-element.25), calls=%async_computation | async-start | bytes 131072 | tf_op jit(solution)/shard_map/all_to_all | solution.py:585
  7.2 1.9 %collective-permute-start = (f32[64,128]{1,0:T(8,128)}, f32[64,128]{1,0:T(8,128)S(1)}, u32[]{:S(2)}, u32[]{:S(2)}) collective-permute-start(f32[64,128]{1,0:T(8,128)} %get-tuple-element.26), channel_id=1, source_target_pairs={{0,8},{16,24},{32,40},{48,56},{64,72},{80,88},{96,104},{112,120},{... | collective-permute-start | bytes 98312 | tf_op jit(solution)/shard_map/ppermute | solution.py:586
  9.2 7.0 %collective-permute-start.1 = (f32[64,128]{1,0:T(8,128)}, f32[64,128]{1,0:T(8,128)S(1)}, u32[]{:S(2)}, u32[]{:S(2)}) collective-permute-start(f32[64,128]{1,0:T(8,128)} %get-tuple-element.27), channel_id=1, source_target_pairs={{8,16},{24,32},{40,48},{56,64},{72,80},{88,96},{104,112},{120,128}... | collective-permute-start | bytes 98312 | tf_op jit(solution)/shard_map/ppermute | solution.py:587
  16.2 0.0 copy-done
  16.2 0.0 copy-done.1
  16.2 0.0 copy-done.8
  16.2 0.0 copy-start.2
  16.3 0.0 copy-start.3
  16.3 0.0 copy-start.4
  16.3 0.0 copy-start.5
  16.3 0.0 copy-start.6
  16.3 1.1 %shard_map.105 = (f32[9,16,128]{2,1,0:T(8,128)S(1)}, bf16[16,128,64]{2,1,0:T(8,128)(2,1)S(1)}, bf16[16,32,128]{2,1,0:T(8,128)(2,1)S(1)}, bf16[16,64,128]{2,1,0:T(8,128)(2,1)S(1)}) custom-call(bf16[128,128]{1,0:T(8,128)(2,1)S(1)} %shard_map.104.unit, f32[3,2048]{1,0:T(4,128)S(1)} %copy-done, f32[16,128]{1,0:T(8,128)S(1)} %bitcast.9, f32[6,2048]{1,0:T(8,128)S(1)} %copy-done.8), custom_call_target="tpu_custom_call" | custom-call | flops 1000000000 | bytes 1000000 | tf_op jit(solution)/shard_map/pallas_call | solution.py:490
  17.4 0.0 collective-permute-done.even_in
  17.4 0.9 %collective-permute-done.1.odd_in = f32[64,128]{1,0:T(8,128)S(1)} collective-permute-done((f32[64,128]{1,0:T(8,128)}, f32[64,128]{1,0:T(8,128)S(1)}, u32[]{:S(2)}, u32[]{:S(2)}) %collective-permute-start.1) | collective-permute-done | bytes 32800 | tf_op jit(solution)/shard_map/ppermute | solution.py:587
  18.3 0.0 all-to-all-done.node_in
  18.3 0.0 copy-done.2
  18.3 0.0 copy-done.3
  18.3 0.0 copy-done.4
  18.3 0.0 copy-done.5
  18.3 15.8 %shard_map.106 = (f32[32,4,128]{2,1,0:T(4,128)}, f32[16,4,128]{2,1,0:T(4,128)S(1)}, f32[16,4,128]{2,1,0:T(4,128)S(1)}, f32[13,16,128]{2,1,0:T(8,128)S(1)}, bf16[...) custom-call(s32[1,16]{1,0:T(1,128)S(1)} %bitcast.14, s32[1,32]{1,0:T(1,128)S(1)} %copy-done.5, ...), custom_call_target="tpu_custom_call" | custom-call | tf_op jit(solution)/shard_map/pallas_call | solution.py:521
  34.2 4.9 %all-to-all-start.1 = ((f32[8,16,128]{2,1,0:T(8,128)}), f32[8,16,128]{2,1,0:T(8,128)S(1)}, u32[]{:S(2)}, u32[]{:S(2)}) async-start(f32[8,16,128]{2,1,0:T(8,128)} %bitcast.4), calls=%async_computation.1 | async-start | bytes 131072 | tf_op jit(solution)/shard_map/all_to_all | solution.py:585
  39.1 0.0 collective-permute-start.2
  39.1 6.0 %collective-permute-start.3 = (f32[64,128]{1,0:T(8,128)S(1)}, f32[64,128]{1,0:T(8,128)S(1)}, u32[]{:S(2)}, u32[]{:S(2)}) collective-permute-start(f32[64,128]{1,0:T(8,128)S(1)} %bitcast.16), channel_id=1, source_target_pairs={{8,16},{24,32},{40,48},{56,64},{72,80},{88,96},{104,112},{120,128}... | collective-permute-start | bytes 98312 | tf_op jit(solution)/shard_map/ppermute | solution.py:587
  45.1 1.4 %shard_map.107.acc_in = f32[16,4,128]{2,1,0:T(4,128)S(1)} custom-call(s32[1,16]{1,0:T(1,128)S(1)} %bitcast.15, f32[13,16,128]{2,1,0:T(8,128)S(1)} %get-tuple-element.28.own_r, bf16[16,32,128]{2,1,0:T(8,128)(2,1)S(1)} %get-tuple-element.29.h, bf16[32,128,256]{2,1,0:T(8,128)(2,1)S(1)} %get-tuple-element.30.w3_local), custom_call_target="tpu_custom_call" | custom-call | flops 1000000000 | bytes 1000000 | tf_op jit(solution)/shard_map/pallas_call | solution.py:552
  46.5 0.0 collective-permute-done.2.even_in
  46.5 0.5 collective-permute-done.3.odd_in
  47.0 0.0 all-to-all-done.1.node_in
  47.0 1.4 %shard_map.108 = (f32[6,2048]{1,0:T(8,128)}, f32[16,128]{1,0:T(8,128)}, f32[3,2048]{1,0:T(4,128)}) custom-call(s32[64]{0:T(128)S(1)} %copy-done.7, f32[13,16,128]{2,1,0:T(8,128)S(1)} %get-tuple-element.28.own_r, f32[16,4,128]{2,1,0:T(4,128)S(1)} %shard_map.107.acc_in, f32[8,16,128]{2,1,0:T(8,128)S(1)} %all-to-all-done.1.node_in, ...), custom_call_target="tpu_custom_call" | custom-call | tf_op jit(solution)/shard_map/pallas_call | solution.py:564
  (4 shorter events, 0.0 us)
Async XLA Ops:
  2.2 14.0 %copy-start = (f32[3,2048]{1,0:T(4,128)S(1)}, f32[3,2048]{1,0:T(4,128)}, u32[]{:S(2)}) copy-start(f32[3,2048]{1,0:T(4,128)} %pos.1) | copy-start | bytes 73732
  2.2 14.0 %copy-start.1 = (f32[2048]{0:T(1024)S(1)}, f32[2048]{0:T(1024)}, u32[]{:S(2)}) copy-start(f32[2048]{0:T(1024)} %param.9) | copy-start | bytes 24580
  2.3 14.0 %copy-start.8 = (f32[6,2048]{1,0:T(8,128)S(1)}, f32[6,2048]{1,0:T(8,128)}, u32[]{:S(2)}) copy-start(f32[6,2048]{1,0:T(8,128)} %metric.1) | copy-start | bytes 147460
  2.3 16.0 %all-to-all-start = ((f32[8,16,128]{2,1,0:T(8,128)}), f32[8,16,128]{2,1,0:T(8,128)S(1)}, u32[]{:S(2)}, u32[]{:S(2)}) async-start(f32[8,16,128]{2,1,0:T(8,128)} %get-tuple-element.25), calls=%async_computation | async-start | bytes 131072 | tf_op jit(solution)/shard_map/all_to_all | solution.py:585
  7.2 10.2 %collective-permute-start = (f32[64,128]{1,0:T(8,128)}, f32[64,128]{1,0:T(8,128)S(1)}, u32[]{:S(2)}, u32[]{:S(2)}) collective-permute-start(f32[64,128]{1,0:T(8,128)} %get-tuple-element.26), channel_id=1, source_target_pairs={{0,8},{16,24},{32,40},{48,56},{64,72},{80,88},{96,104},{112,120},{... | collective-permute-start | bytes 98312 | tf_op jit(solution)/shard_map/ppermute | solution.py:586
  9.2 9.1 %collective-permute-start.1 = (f32[64,128]{1,0:T(8,128)}, f32[64,128]{1,0:T(8,128)S(1)}, u32[]{:S(2)}, u32[]{:S(2)}) collective-permute-start(f32[64,128]{1,0:T(8,128)} %get-tuple-element.27), channel_id=1, source_target_pairs={{8,16},{24,32},{40,48},{56,64},{72,80},{88,96},{104,112},{120,128}... | collective-permute-start | bytes 98312 | tf_op jit(solution)/shard_map/ppermute | solution.py:587
  16.2 2.0 %copy-start.2 = (f32[2048]{0:T(1024)S(1)}, f32[2048]{0:T(1024)}, u32[]{:S(2)}) copy-start(f32[2048]{0:T(1024)} %param.11) | copy-start | bytes 24580
  16.3 2.0 %copy-start.3 = (s32[1,8,2]{1,2,0:T(2,128)S(1)}, s32[1,8,2]{1,2,0:T(2,128)}, u32[]{:S(2)}) copy-start(s32[1,8,2]{1,2,0:T(2,128)} %param.14) | copy-start | bytes 196
  16.3 2.0 %copy-start.4 = (s32[1,2,8]{2,1,0:T(2,128)S(1)}, s32[1,2,8]{2,1,0:T(2,128)}, u32[]{:S(2)}) copy-start(s32[1,2,8]{2,1,0:T(2,128)} %ds.1) | copy-start | bytes 196
  16.3 2.0 %copy-start.5 = (s32[1,32]{1,0:T(1,128)S(1)}, s32[1,32]{1,0:T(1,128)}, u32[]{:S(2)}) copy-start(s32[1,32]{1,0:T(1,128)} %gp.1) | copy-start | bytes 388
  16.3 2.0 %copy-start.6 = (s32[16,1]{0,1:T(1,128)S(1)}, s32[16,1]{0,1:T(1,128)}, u32[]{:S(2)}) copy-start(s32[16,1]{0,1:T(1,128)} %param.12) | copy-start | bytes 196
  34.1 12.9 %copy-start.7 = (s32[64]{0:T(128)S(1)}, s32[64]{0:T(128)}, u32[]{:S(2)}) copy-start(s32[64]{0:T(128)} %get-tuple-element.20.sent) | copy-start | bytes 772
  34.2 12.8 %all-to-all-start.1 = ((f32[8,16,128]{2,1,0:T(8,128)}), f32[8,16,128]{2,1,0:T(8,128)S(1)}, u32[]{:S(2)}, u32[]{:S(2)}) async-start(f32[8,16,128]{2,1,0:T(8,128)} %bitcast.4), calls=%async_computation.1 | async-start | bytes 131072 | tf_op jit(solution)/shard_map/all_to_all | solution.py:585
  39.1 7.4 %collective-permute-start.2 = (f32[64,128]{1,0:T(8,128)S(1)}, f32[64,128]{1,0:T(8,128)S(1)}, u32[]{:S(2)}, u32[]{:S(2)}) collective-permute-start(f32[64,128]{1,0:T(8,128)S(1)} %bitcast.17), channel_id=1, source_target_pairs={{0,8},{16,24},{32,40},{48,56},{64,72},{80,88},{96,104},{112,120},{... | collective-permute-start | bytes 98312 | tf_op jit(solution)/shard_map/ppermute | solution.py:586
  39.1 7.9 %collective-permute-start.3 = (f32[64,128]{1,0:T(8,128)S(1)}, f32[64,128]{1,0:T(8,128)S(1)}, u32[]{:S(2)}, u32[]{:S(2)}) collective-permute-start(f32[64,128]{1,0:T(8,128)S(1)} %bitcast.16), channel_id=1, source_target_pairs={{8,16},{24,32},{40,48},{56,64},{72,80},{88,96},{104,112},{120,128}... | collective-permute-start | bytes 98312 | tf_op jit(solution)/shard_map/ppermute | solution.py:587

commit v3 on v2

--- a/solution.py
+++ b/solution.py
@@ -113,8 +113,7 @@
 
 
 def reciprocal(value):
-    guess = pl.reciprocal(value, approx=True)
-    return guess * (2.0 - value * guess)
+    return pl.reciprocal(value, approx=True)
 
 
 def unit_kernel(unit):

time: 48.8 us -> 47.6 us (0.975)
  Pallas kernels: 21.4 us -> 20.1 us
    pallas_call x1, Pallas kernels: 15.8 us -> 14.6 us  [main_call(): pl.pallas_call(main_kernel, out_shape=(shape(32, 4, W), shape(16, 4, W),...]
where the time goes in v3:
time: 47.6 us; the launch traced here: 47.2 us
  starting transfers between devices  24.9 us (52%)
  Pallas kernels  20.1 us (42%)
  waiting for transfers between devices  1.35 us (3%)
  between operations  0.81 us (2%)
    pallas_call x1, Pallas kernels, main_call(): pl.pallas_call(main_kernel, out_shape=(shape(32, 4, W), shape(16, 4, W),...  14.6 us
    ppermute x2, starting transfers between devices, exchange(): lax.ppermute(odd, 'dom', swaps(1))  13 us
    all_to_all x2, starting transfers between devices, exchange(): lax.all_to_all(node, 'node', split_axis=0, concat_axis=0, tiled=True)  9.91 us
    ppermute x2, starting transfers between devices, exchange(): lax.ppermute(even, 'dom', swaps(0))  1.92 us
    pallas_call x1, Pallas kernels, gather_call(): pl.pallas_call(gather_kernel, out_shape=(shape(NODE, 16, W), shape(64, W)...  1.6 us
    pallas_call x1, Pallas kernels, final_call(): pl.pallas_call(final_kernel, out_shape=(shape(6, NB * W), shape(NB, W), s...  1.45 us
    pallas_call x1, Pallas kernels, rest_call(): pl.pallas_call(rest_kernel, out_shape=shape(NB, 4, W), in_specs=[SMEM] +...  1.39 us
    ppermute x2, waiting for transfers between devices, exchange(): lax.ppermute(odd, 'dom', swaps(1))  1.34 us
  transfers between devices with their start and end apart: 6, of which 2 were waited for; matrix products, arithmetic and copies ran while one was open for 0% of the time, Pallas kernels for 5%

profile of v3, /device:TPU:26, one launch (start us, length us, event | category | flops | bytes accessed | tf_op | source)
XLA Modules:
  0.0 47.2 jit_solution(14689408621452355943)
XLA Ops:
  0.6 1.6 %shard_map.103 = (f32[8,16,128]{2,1,0:T(8,128)}, f32[64,128]{1,0:T(8,128)}, f32[64,128]{1,0:T(8,128)}, s32[64]{0:T(128)}) custom-call(s32[1,32]{1,0:T(1,128)} %gp.1, s32[1,2,8]{2,1,0:T(2,128)} %bitcast.12, s32[1,2,8]{2,1,0:T(2,128)} %ds.1, f32[3,2048]{1,0:T(4,128)} %pos.1, f32[16,128]{1,0:T(8,128)} %bitcast.8), custom_call_target="tpu_custom_call" | custom-call | tf_op jit(solution)/shard_map/pallas_call | solution.py:470
  2.2 0.0 copy-start
  2.2 0.0 copy-start.1
  2.3 0.0 copy-start.8
  2.3 5.0 %all-to-all-start = ((f32[8,16,128]{2,1,0:T(8,128)}), f32[8,16,128]{2,1,0:T(8,128)S(1)}, u32[]{:S(2)}, u32[]{:S(2)}) async-start(f32[8,16,128]{2,1,0:T(8,128)} %get-tuple-element.25), calls=%async_computation | async-start | bytes 131072 | tf_op jit(solution)/shard_map/all_to_all | solution.py:584
  7.2 1.9 %collective-permute-start = (f32[64,128]{1,0:T(8,128)}, f32[64,128]{1,0:T(8,128)S(1)}, u32[]{:S(2)}, u32[]{:S(2)}) collective-permute-start(f32[64,128]{1,0:T(8,128)} %get-tuple-element.26), channel_id=1, source_target_pairs={{0,8},{16,24},{32,40},{48,56},{64,72},{80,88},{96,104},{112,120},{... | collective-permute-start | bytes 98312 | tf_op jit(solution)/shard_map/ppermute | solution.py:585
  9.2 7.0 %collective-permute-start.1 = (f32[64,128]{1,0:T(8,128)}, f32[64,128]{1,0:T(8,128)S(1)}, u32[]{:S(2)}, u32[]{:S(2)}) collective-permute-start(f32[64,128]{1,0:T(8,128)} %get-tuple-element.27), channel_id=1, source_target_pairs={{8,16},{24,32},{40,48},{56,64},{72,80},{88,96},{104,112},{120,128}... | collective-permute-start | bytes 98312 | tf_op jit(solution)/shard_map/ppermute | solution.py:586
  16.2 0.0 copy-done
  16.2 0.0 copy-done.1
  16.2 0.0 copy-done.8
  16.2 0.0 copy-start.2
  16.3 0.0 copy-start.3
  16.3 0.0 copy-start.4
  16.3 0.0 copy-start.5
  16.3 0.0 copy-start.6
  16.3 1.1 %shard_map.105 = (f32[9,16,128]{2,1,0:T(8,128)S(1)}, bf16[16,128,64]{2,1,0:T(8,128)(2,1)S(1)}, bf16[16,32,128]{2,1,0:T(8,128)(2,1)S(1)}, bf16[16,64,128]{2,1,0:T(8,128)(2,1)S(1)}) custom-call(bf16[128,128]{1,0:T(8,128)(2,1)S(1)} %shard_map.104.unit, f32[3,2048]{1,0:T(4,128)S(1)} %copy-done, f32[16,128]{1,0:T(8,128)S(1)} %bitcast.9, f32[6,2048]{1,0:T(8,128)S(1)} %copy-done.8), custom_call_target="tpu_custom_call" | custom-call | flops 1000000000 | bytes 1000000 | tf_op jit(solution)/shard_map/pallas_call | solution.py:489
  17.4 0.0 collective-permute-done.even_in
  17.4 0.9 %collective-permute-done.1.odd_in = f32[64,128]{1,0:T(8,128)S(1)} collective-permute-done((f32[64,128]{1,0:T(8,128)}, f32[64,128]{1,0:T(8,128)S(1)}, u32[]{:S(2)}, u32[]{:S(2)}) %collective-permute-start.1) | collective-permute-done | bytes 32800 | tf_op jit(solution)/shard_map/ppermute | solution.py:586
  18.3 0.0 all-to-all-done.node_in
  18.3 0.0 copy-done.2
  18.3 0.0 copy-done.3
  18.3 0.0 copy-done.4
  18.3 0.0 copy-done.5
  18.3 14.6 %shard_map.106 = (f32[32,4,128]{2,1,0:T(4,128)}, f32[16,4,128]{2,1,0:T(4,128)S(1)}, f32[16,4,128]{2,1,0:T(4,128)S(1)}, f32[13,16,128]{2,1,0:T(8,128)S(1)}, bf16[...) custom-call(s32[1,16]{1,0:T(1,128)S(1)} %bitcast.14, s32[1,32]{1,0:T(1,128)S(1)} %copy-done.5, ...), custom_call_target="tpu_custom_call" | custom-call | tf_op jit(solution)/shard_map/pallas_call | solution.py:520
  32.9 4.9 %all-to-all-start.1 = ((f32[8,16,128]{2,1,0:T(8,128)}), f32[8,16,128]{2,1,0:T(8,128)S(1)}, u32[]{:S(2)}, u32[]{:S(2)}) async-start(f32[8,16,128]{2,1,0:T(8,128)} %bitcast.4), calls=%async_computation.1 | async-start | bytes 131072 | tf_op jit(solution)/shard_map/all_to_all | solution.py:584
  37.9 0.0 collective-permute-start.2
  37.9 6.0 %collective-permute-start.3 = (f32[64,128]{1,0:T(8,128)S(1)}, f32[64,128]{1,0:T(8,128)S(1)}, u32[]{:S(2)}, u32[]{:S(2)}) collective-permute-start(f32[64,128]{1,0:T(8,128)S(1)} %bitcast.16), channel_id=1, source_target_pairs={{8,16},{24,32},{40,48},{56,64},{72,80},{88,96},{104,112},{120,128}... | collective-permute-start | bytes 98312 | tf_op jit(solution)/shard_map/ppermute | solution.py:586
  43.9 1.4 %shard_map.107.acc_in = f32[16,4,128]{2,1,0:T(4,128)S(1)} custom-call(s32[1,16]{1,0:T(1,128)S(1)} %bitcast.15, f32[13,16,128]{2,1,0:T(8,128)S(1)} %get-tuple-element.28.own_r, bf16[16,32,128]{2,1,0:T(8,128)(2,1)S(1)} %get-tuple-element.29.h, bf16[32,128,256]{2,1,0:T(8,128)(2,1)S(1)} %get-tuple-element.30.w3_local), custom_call_target="tpu_custom_call" | custom-call | flops 1000000000 | bytes 1000000 | tf_op jit(solution)/shard_map/pallas_call | solution.py:551
  45.3 0.0 collective-permute-done.2.even_in
  45.3 0.5 collective-permute-done.3.odd_in
  45.8 0.0 all-to-all-done.1.node_in
  45.8 1.5 %shard_map.108 = (f32[6,2048]{1,0:T(8,128)}, f32[16,128]{1,0:T(8,128)}, f32[3,2048]{1,0:T(4,128)}) custom-call(s32[64]{0:T(128)S(1)} %copy-done.7, f32[13,16,128]{2,1,0:T(8,128)S(1)} %get-tuple-element.28.own_r, f32[16,4,128]{2,1,0:T(4,128)S(1)} %shard_map.107.acc_in, f32[8,16,128]{2,1,0:T(8,128)S(1)} %all-to-all-done.1.node_in, ...), custom_call_target="tpu_custom_call" | custom-call | tf_op jit(solution)/shard_map/pallas_call | solution.py:563
  (4 shorter events, 0.0 us)
Async XLA Ops:
  2.2 14.0 %copy-start = (f32[3,2048]{1,0:T(4,128)S(1)}, f32[3,2048]{1,0:T(4,128)}, u32[]{:S(2)}) copy-start(f32[3,2048]{1,0:T(4,128)} %pos.1) | copy-start | bytes 73732
  2.2 14.0 %copy-start.1 = (f32[2048]{0:T(1024)S(1)}, f32[2048]{0:T(1024)}, u32[]{:S(2)}) copy-start(f32[2048]{0:T(1024)} %param.9) | copy-start | bytes 24580
  2.3 14.0 %copy-start.8 = (f32[6,2048]{1,0:T(8,128)S(1)}, f32[6,2048]{1,0:T(8,128)}, u32[]{:S(2)}) copy-start(f32[6,2048]{1,0:T(8,128)} %metric.1) | copy-start | bytes 147460
  2.3 16.0 %all-to-all-start = ((f32[8,16,128]{2,1,0:T(8,128)}), f32[8,16,128]{2,1,0:T(8,128)S(1)}, u32[]{:S(2)}, u32[]{:S(2)}) async-start(f32[8,16,128]{2,1,0:T(8,128)} %get-tuple-element.25), calls=%async_computation | async-start | bytes 131072 | tf_op jit(solution)/shard_map/all_to_all | solution.py:584
  7.2 10.2 %collective-permute-start = (f32[64,128]{1,0:T(8,128)}, f32[64,128]{1,0:T(8,128)S(1)}, u32[]{:S(2)}, u32[]{:S(2)}) collective-permute-start(f32[64,128]{1,0:T(8,128)} %get-tuple-element.26), channel_id=1, source_target_pairs={{0,8},{16,24},{32,40},{48,56},{64,72},{80,88},{96,104},{112,120},{... | collective-permute-start | bytes 98312 | tf_op jit(solution)/shard_map/ppermute | solution.py:585
  9.2 9.1 %collective-permute-start.1 = (f32[64,128]{1,0:T(8,128)}, f32[64,128]{1,0:T(8,128)S(1)}, u32[]{:S(2)}, u32[]{:S(2)}) collective-permute-start(f32[64,128]{1,0:T(8,128)} %get-tuple-element.27), channel_id=1, source_target_pairs={{8,16},{24,32},{40,48},{56,64},{72,80},{88,96},{104,112},{120,128}... | collective-permute-start | bytes 98312 | tf_op jit(solution)/shard_map/ppermute | solution.py:586
  16.2 2.0 %copy-start.2 = (f32[2048]{0:T(1024)S(1)}, f32[2048]{0:T(1024)}, u32[]{:S(2)}) copy-start(f32[2048]{0:T(1024)} %param.11) | copy-start | bytes 24580
  16.3 2.0 %copy-start.3 = (s32[1,8,2]{1,2,0:T(2,128)S(1)}, s32[1,8,2]{1,2,0:T(2,128)}, u32[]{:S(2)}) copy-start(s32[1,8,2]{1,2,0:T(2,128)} %param.14) | copy-start | bytes 196
  16.3 2.0 %copy-start.4 = (s32[1,2,8]{2,1,0:T(2,128)S(1)}, s32[1,2,8]{2,1,0:T(2,128)}, u32[]{:S(2)}) copy-start(s32[1,2,8]{2,1,0:T(2,128)} %ds.1) | copy-start | bytes 196
  16.3 2.0 %copy-start.5 = (s32[1,32]{1,0:T(1,128)S(1)}, s32[1,32]{1,0:T(1,128)}, u32[]{:S(2)}) copy-start(s32[1,32]{1,0:T(1,128)} %gp.1) | copy-start | bytes 388
  16.3 2.0 %copy-start.6 = (s32[16,1]{0,1:T(1,128)S(1)}, s32[16,1]{0,1:T(1,128)}, u32[]{:S(2)}) copy-start(s32[16,1]{0,1:T(1,128)} %param.12) | copy-start | bytes 196
  32.9 12.9 %copy-start.7 = (s32[64]{0:T(128)S(1)}, s32[64]{0:T(128)}, u32[]{:S(2)}) copy-start(s32[64]{0:T(128)} %get-tuple-element.20.sent) | copy-start | bytes 772
  32.9 12.8 %all-to-all-start.1 = ((f32[8,16,128]{2,1,0:T(8,128)}), f32[8,16,128]{2,1,0:T(8,128)S(1)}, u32[]{:S(2)}, u32[]{:S(2)}) async-start(f32[8,16,128]{2,1,0:T(8,128)} %bitcast.4), calls=%async_computation.1 | async-start | bytes 131072 | tf_op jit(solution)/shard_map/all_to_all | solution.py:584
  37.9 7.4 %collective-permute-start.2 = (f32[64,128]{1,0:T(8,128)S(1)}, f32[64,128]{1,0:T(8,128)S(1)}, u32[]{:S(2)}, u32[]{:S(2)}) collective-permute-start(f32[64,128]{1,0:T(8,128)S(1)} %bitcast.17), channel_id=1, source_target_pairs={{0,8},{16,24},{32,40},{48,56},{64,72},{80,88},{96,104},{112,120},{... | collective-permute-start | bytes 98312 | tf_op jit(solution)/shard_map/ppermute | solution.py:585
  37.9 7.9 %collective-permute-start.3 = (f32[64,128]{1,0:T(8,128)S(1)}, f32[64,128]{1,0:T(8,128)S(1)}, u32[]{:S(2)}, u32[]{:S(2)}) collective-permute-start(f32[64,128]{1,0:T(8,128)S(1)} %bitcast.16), channel_id=1, source_target_pairs={{8,16},{24,32},{40,48},{56,64},{72,80},{88,96},{104,112},{120,128}... | collective-permute-start | bytes 98312 | tf_op jit(solution)/shard_map/ppermute | solution.py:586

commit v4 on v3

--- a/solution.py
+++ b/solution.py
@@ -391,8 +391,10 @@
     for t in range(16, 32):
         back[variable_partner(t) - NB] = turn_back(h[own[t]], w3[32 + t])
     for e in range(NB):
-        for c in range(1, 4):
-            back[part[4 * e + c] - NB] = turn_back(h[e], w3[3 * e + c - 1])
+        rows = [slice(3 * e + c, 3 * e + c + 1) for c in range(3)]
+        out = turn_back(h[e], w3[3 * e : 3 * e + 3].reshape(3 * W, 2 * W))
+        for c in range(3):
+            back[part[4 * e + 1 + c] - NB] = out[:, c * W : (c + 1) * W]
     for first, count, view, out in (
         (0, 32, node_view, node_out),
         (32, 16, even_view, even_out),

time: 47.6 us -> 47.5 us (level)
  no operation moved by 1% of the time
where the time goes in v4:
time: 47.5 us; the launch traced here: 47.1 us
  starting transfers between devices  24.9 us (52%)
  Pallas kernels  20 us (42%)
  waiting for transfers between devices  1.36 us (3%)
  between operations  0.81 us (2%)
    pallas_call x1, Pallas kernels, main_call(): pl.pallas_call(main_kernel, out_shape=(shape(32, 4, W), shape(16, 4, W),...  14.4 us
    ppermute x2, starting transfers between devices, exchange(): lax.ppermute(odd, 'dom', swaps(1))  13 us
    all_to_all x2, starting transfers between devices, exchange(): lax.all_to_all(node, 'node', split_axis=0, concat_axis=0, tiled=True)  9.92 us
    ppermute x2, starting transfers between devices, exchange(): lax.ppermute(even, 'dom', swaps(0))  1.92 us
    pallas_call x1, Pallas kernels, gather_call(): pl.pallas_call(gather_kernel, out_shape=(shape(NODE, 16, W), shape(64, W)...  1.6 us
    pallas_call x1, Pallas kernels, final_call(): pl.pallas_call(final_kernel, out_shape=(shape(6, NB * W), shape(NB, W), s...  1.45 us
    pallas_call x1, Pallas kernels, rest_call(): pl.pallas_call(rest_kernel, out_shape=shape(NB, 4, W), in_specs=[SMEM] +...  1.39 us
    ppermute x2, waiting for transfers between devices, exchange(): lax.ppermute(odd, 'dom', swaps(1))  1.34 us
  transfers between devices with their start and end apart: 6, of which 2 were waited for; matrix products, arithmetic and copies ran while one was open for 0% of the time, Pallas kernels for 5%

profile of v4, /device:TPU:26, one launch (start us, length us, event | category | flops | bytes accessed | tf_op | source)
XLA Modules:
  0.0 47.1 jit_solution(6036815811911915630)
XLA Ops:
  0.6 1.6 %shard_map.103 = (f32[8,16,128]{2,1,0:T(8,128)}, f32[64,128]{1,0:T(8,128)}, f32[64,128]{1,0:T(8,128)}, s32[64]{0:T(128)}) custom-call(s32[1,32]{1,0:T(1,128)} %gp.1, s32[1,2,8]{2,1,0:T(2,128)} %bitcast.12, s32[1,2,8]{2,1,0:T(2,128)} %ds.1, f32[3,2048]{1,0:T(4,128)} %pos.1, f32[16,128]{1,0:T(8,128)} %bitcast.8), custom_call_target="tpu_custom_call" | custom-call | tf_op jit(solution)/shard_map/pallas_call | solution.py:472
  2.2 0.0 copy-start
  2.2 0.0 copy-start.1
  2.3 0.0 copy-start.8
  2.3 5.0 %all-to-all-start = ((f32[8,16,128]{2,1,0:T(8,128)}), f32[8,16,128]{2,1,0:T(8,128)S(1)}, u32[]{:S(2)}, u32[]{:S(2)}) async-start(f32[8,16,128]{2,1,0:T(8,128)} %get-tuple-element.25), calls=%async_computation | async-start | bytes 131072 | tf_op jit(solution)/shard_map/all_to_all | solution.py:586
  7.2 1.9 %collective-permute-start = (f32[64,128]{1,0:T(8,128)}, f32[64,128]{1,0:T(8,128)S(1)}, u32[]{:S(2)}, u32[]{:S(2)}) collective-permute-start(f32[64,128]{1,0:T(8,128)} %get-tuple-element.26), channel_id=1, source_target_pairs={{0,8},{16,24},{32,40},{48,56},{64,72},{80,88},{96,104},{112,120},{... | collective-permute-start | bytes 98312 | tf_op jit(solution)/shard_map/ppermute | solution.py:587
  9.2 7.0 %collective-permute-start.1 = (f32[64,128]{1,0:T(8,128)}, f32[64,128]{1,0:T(8,128)S(1)}, u32[]{:S(2)}, u32[]{:S(2)}) collective-permute-start(f32[64,128]{1,0:T(8,128)} %get-tuple-element.27), channel_id=1, source_target_pairs={{8,16},{24,32},{40,48},{56,64},{72,80},{88,96},{104,112},{120,128}... | collective-permute-start | bytes 98312 | tf_op jit(solution)/shard_map/ppermute | solution.py:588
  16.2 0.0 copy-done
  16.2 0.0 copy-done.1
  16.2 0.0 copy-done.8
  16.2 0.0 copy-start.2
  16.3 0.0 copy-start.3
  16.3 0.0 copy-start.4
  16.3 0.0 copy-start.5
  16.3 0.0 copy-start.6
  16.3 1.1 %shard_map.105 = (f32[9,16,128]{2,1,0:T(8,128)S(1)}, bf16[16,128,64]{2,1,0:T(8,128)(2,1)S(1)}, bf16[16,32,128]{2,1,0:T(8,128)(2,1)S(1)}, bf16[16,64,128]{2,1,0:T(8,128)(2,1)S(1)}) custom-call(bf16[128,128]{1,0:T(8,128)(2,1)S(1)} %shard_map.104.unit, f32[3,2048]{1,0:T(4,128)S(1)} %copy-done, f32[16,128]{1,0:T(8,128)S(1)} %bitcast.9, f32[6,2048]{1,0:T(8,128)S(1)} %copy-done.8), custom_call_target="tpu_custom_call" | custom-call | flops 1000000000 | bytes 1000000 | tf_op jit(solution)/shard_map/pallas_call | solution.py:491
  17.4 0.0 collective-permute-done.even_in
  17.4 0.9 %collective-permute-done.1.odd_in = f32[64,128]{1,0:T(8,128)S(1)} collective-permute-done((f32[64,128]{1,0:T(8,128)}, f32[64,128]{1,0:T(8,128)S(1)}, u32[]{:S(2)}, u32[]{:S(2)}) %collective-permute-start.1) | collective-permute-done | bytes 32800 | tf_op jit(solution)/shard_map/ppermute | solution.py:588
  18.3 0.0 all-to-all-done.node_in
  18.3 0.0 copy-done.2
  18.3 0.0 copy-done.3
  18.3 0.0 copy-done.4
  18.3 0.0 copy-done.5
  18.3 14.4 %shard_map.106 = (f32[32,4,128]{2,1,0:T(4,128)}, f32[16,4,128]{2,1,0:T(4,128)S(1)}, f32[16,4,128]{2,1,0:T(4,128)S(1)}, f32[13,16,128]{2,1,0:T(8,128)S(1)}, bf16[...) custom-call(s32[1,16]{1,0:T(1,128)S(1)} %bitcast.14, s32[1,32]{1,0:T(1,128)S(1)} %copy-done.5, ...), custom_call_target="tpu_custom_call" | custom-call | tf_op jit(solution)/shard_map/pallas_call | solution.py:522
  32.8 4.9 %all-to-all-start.1 = ((f32[8,16,128]{2,1,0:T(8,128)}), f32[8,16,128]{2,1,0:T(8,128)S(1)}, u32[]{:S(2)}, u32[]{:S(2)}) async-start(f32[8,16,128]{2,1,0:T(8,128)} %bitcast.4), calls=%async_computation.1 | async-start | bytes 131072 | tf_op jit(solution)/shard_map/all_to_all | solution.py:586
  37.7 0.0 collective-permute-start.2
  37.7 6.0 %collective-permute-start.3 = (f32[64,128]{1,0:T(8,128)S(1)}, f32[64,128]{1,0:T(8,128)S(1)}, u32[]{:S(2)}, u32[]{:S(2)}) collective-permute-start(f32[64,128]{1,0:T(8,128)S(1)} %bitcast.16), channel_id=1, source_target_pairs={{8,16},{24,32},{40,48},{56,64},{72,80},{88,96},{104,112},{120,128}... | collective-permute-start | bytes 98312 | tf_op jit(solution)/shard_map/ppermute | solution.py:588
  43.7 1.4 %shard_map.107.acc_in = f32[16,4,128]{2,1,0:T(4,128)S(1)} custom-call(s32[1,16]{1,0:T(1,128)S(1)} %bitcast.15, f32[13,16,128]{2,1,0:T(8,128)S(1)} %get-tuple-element.28.own_r, bf16[16,32,128]{2,1,0:T(8,128)(2,1)S(1)} %get-tuple-element.29.h, bf16[32,128,256]{2,1,0:T(8,128)(2,1)S(1)} %get-tuple-element.30.w3_local), custom_call_target="tpu_custom_call" | custom-call | flops 1000000000 | bytes 1000000 | tf_op jit(solution)/shard_map/pallas_call | solution.py:553
  45.1 0.0 collective-permute-done.2.even_in
  45.1 0.5 %collective-permute-done.3.odd_in = f32[64,128]{1,0:T(8,128)S(1)} collective-permute-done((f32[64,128]{1,0:T(8,128)S(1)}, f32[64,128]{1,0:T(8,128)S(1)}, u32[]{:S(2)}, u32[]{:S(2)}) %collective-permute-start.3) | collective-permute-done | bytes 32800 | tf_op jit(solution)/shard_map/ppermute | solution.py:588
  45.6 0.0 all-to-all-done.1.node_in
  45.6 1.5 %shard_map.108 = (f32[6,2048]{1,0:T(8,128)}, f32[16,128]{1,0:T(8,128)}, f32[3,2048]{1,0:T(4,128)}) custom-call(s32[64]{0:T(128)S(1)} %copy-done.7, f32[13,16,128]{2,1,0:T(8,128)S(1)} %get-tuple-element.28.own_r, f32[16,4,128]{2,1,0:T(4,128)S(1)} %shard_map.107.acc_in, f32[8,16,128]{2,1,0:T(8,128)S(1)} %all-to-all-done.1.node_in, ...), custom_call_target="tpu_custom_call" | custom-call | tf_op jit(solution)/shard_map/pallas_call | solution.py:565
  (4 shorter events, 0.0 us)
Async XLA Ops:
  2.2 14.0 %copy-start = (f32[3,2048]{1,0:T(4,128)S(1)}, f32[3,2048]{1,0:T(4,128)}, u32[]{:S(2)}) copy-start(f32[3,2048]{1,0:T(4,128)} %pos.1) | copy-start | bytes 73732
  2.2 14.0 %copy-start.1 = (f32[2048]{0:T(1024)S(1)}, f32[2048]{0:T(1024)}, u32[]{:S(2)}) copy-start(f32[2048]{0:T(1024)} %param.9) | copy-start | bytes 24580
  2.3 14.0 %copy-start.8 = (f32[6,2048]{1,0:T(8,128)S(1)}, f32[6,2048]{1,0:T(8,128)}, u32[]{:S(2)}) copy-start(f32[6,2048]{1,0:T(8,128)} %metric.1) | copy-start | bytes 147460
  2.3 16.0 %all-to-all-start = ((f32[8,16,128]{2,1,0:T(8,128)}), f32[8,16,128]{2,1,0:T(8,128)S(1)}, u32[]{:S(2)}, u32[]{:S(2)}) async-start(f32[8,16,128]{2,1,0:T(8,128)} %get-tuple-element.25), calls=%async_computation | async-start | bytes 131072 | tf_op jit(solution)/shard_map/all_to_all | solution.py:586
  7.2 10.2 %collective-permute-start = (f32[64,128]{1,0:T(8,128)}, f32[64,128]{1,0:T(8,128)S(1)}, u32[]{:S(2)}, u32[]{:S(2)}) collective-permute-start(f32[64,128]{1,0:T(8,128)} %get-tuple-element.26), channel_id=1, source_target_pairs={{0,8},{16,24},{32,40},{48,56},{64,72},{80,88},{96,104},{112,120},{... | collective-permute-start | bytes 98312 | tf_op jit(solution)/shard_map/ppermute | solution.py:587
  9.2 9.1 %collective-permute-start.1 = (f32[64,128]{1,0:T(8,128)}, f32[64,128]{1,0:T(8,128)S(1)}, u32[]{:S(2)}, u32[]{:S(2)}) collective-permute-start(f32[64,128]{1,0:T(8,128)} %get-tuple-element.27), channel_id=1, source_target_pairs={{8,16},{24,32},{40,48},{56,64},{72,80},{88,96},{104,112},{120,128}... | collective-permute-start | bytes 98312 | tf_op jit(solution)/shard_map/ppermute | solution.py:588
  16.2 2.0 %copy-start.2 = (f32[2048]{0:T(1024)S(1)}, f32[2048]{0:T(1024)}, u32[]{:S(2)}) copy-start(f32[2048]{0:T(1024)} %param.11) | copy-start | bytes 24580
  16.3 2.0 %copy-start.3 = (s32[1,8,2]{1,2,0:T(2,128)S(1)}, s32[1,8,2]{1,2,0:T(2,128)}, u32[]{:S(2)}) copy-start(s32[1,8,2]{1,2,0:T(2,128)} %param.14) | copy-start | bytes 196
  16.3 2.0 %copy-start.4 = (s32[1,2,8]{2,1,0:T(2,128)S(1)}, s32[1,2,8]{2,1,0:T(2,128)}, u32[]{:S(2)}) copy-start(s32[1,2,8]{2,1,0:T(2,128)} %ds.1) | copy-start | bytes 196
  16.3 2.0 %copy-start.5 = (s32[1,32]{1,0:T(1,128)S(1)}, s32[1,32]{1,0:T(1,128)}, u32[]{:S(2)}) copy-start(s32[1,32]{1,0:T(1,128)} %gp.1) | copy-start | bytes 388
  16.3 2.0 %copy-start.6 = (s32[16,1]{0,1:T(1,128)S(1)}, s32[16,1]{0,1:T(1,128)}, u32[]{:S(2)}) copy-start(s32[16,1]{0,1:T(1,128)} %param.12) | copy-start | bytes 196
  32.8 12.9 %copy-start.7 = (s32[64]{0:T(128)S(1)}, s32[64]{0:T(128)}, u32[]{:S(2)}) copy-start(s32[64]{0:T(128)} %get-tuple-element.20.sent) | copy-start | bytes 772
  32.8 12.9 %all-to-all-start.1 = ((f32[8,16,128]{2,1,0:T(8,128)}), f32[8,16,128]{2,1,0:T(8,128)S(1)}, u32[]{:S(2)}, u32[]{:S(2)}) async-start(f32[8,16,128]{2,1,0:T(8,128)} %bitcast.4), calls=%async_computation.1 | async-start | bytes 131072 | tf_op jit(solution)/shard_map/all_to_all | solution.py:586
  37.7 7.4 %collective-permute-start.2 = (f32[64,128]{1,0:T(8,128)S(1)}, f32[64,128]{1,0:T(8,128)S(1)}, u32[]{:S(2)}, u32[]{:S(2)}) collective-permute-start(f32[64,128]{1,0:T(8,128)S(1)} %bitcast.17), channel_id=1, source_target_pairs={{0,8},{16,24},{32,40},{48,56},{64,72},{80,88},{96,104},{112,120},{... | collective-permute-start | bytes 98312 | tf_op jit(solution)/shard_map/ppermute | solution.py:587
  37.7 7.9 %collective-permute-start.3 = (f32[64,128]{1,0:T(8,128)S(1)}, f32[64,128]{1,0:T(8,128)S(1)}, u32[]{:S(2)}, u32[]{:S(2)}) collective-permute-start(f32[64,128]{1,0:T(8,128)S(1)} %bitcast.16), channel_id=1, source_target_pairs={{8,16},{24,32},{40,48},{56,64},{72,80},{88,96},{104,112},{120,128}... | collective-permute-start | bytes 98312 | tf_op jit(solution)/shard_map/ppermute | solution.py:588
